TPU v7x, 768 devices: a whole 4x8x12 slice. The times are simulated.
768 devices in a mesh: rows: 384 (over x, y, z), grp: 2 (over core).
Axes of the slice: x: 4, y: 8, z: 12, core: 2. Of those that a mesh axis runs over, the one named last changes fastest.
Arguments:
- a_tiles: bfloat16 [6144, 15, 128, 128], P(('rows', 'grp')), may hold values from -1 to 1
- a_cols: int32 [6144, 15], P(('rows', 'grp')), may hold values from 0 to 15
- a_count: int32 [768, 8], P(('rows', 'grp')), may hold values from 1 to 15, 40 in all within a row
- send_lists: int32 [768, 8], P(('rows', 'grp')), may hold values from 0 to 7
- ghost_cols: int32 [768, 8], P(('rows', 'grp')), may hold values from 0 to 5
- cmap: int32 [6144], P(('rows', 'grp')), may hold values from 0 to 1
- p_tiles: bfloat16 [6144, 128, 128], P(('rows', 'grp')), may hold values from -0.5 to 0.5
- x_start: float32 [768, 128], P(('rows', 'grp')), may hold values from -6 to 6
- coarse_rhs: float32 [768, 128], P(('rows', 'grp')), may hold values from -24 to 24
Outputs:
- coarse_op: float32 [768, 128, 768], P(('rows', 'grp'))
- coarse_sol: float32 [768, 128], P(('rows', 'grp'))
Inputs may be any that keep to these rules, and one draw needn't show every extreme that they name: `a_count`: each device's 8 counts sum to 40 and the largest of them is exactly 15. `a_cols`: slots at or beyond a row's count carry no entry; values 0 to 7 are own blocks, 8 to 11 the lower ghosts, the rest the upper ghosts.
All inputs are finite; a program needn't handle non-finite values.
Results may differ from a plain program's by a relative error of at most 0.003.
Values may be sent and summed in bfloat16 or wider, within the bound.
No kernel may reach another device: no remote copies, remote signals or barrier semaphores. Data moves between devices by JAX's collectives and lax.ppermute only.
A program may use at most 64 MiB of HBM per device.

v0:
```python
import jax
import jax.numpy as jnp
from jax import lax
from jax.sharding import PartitionSpec as P

B = 128
K = 15
G = 4
CC = 2


def extended_2(shard, sides, width):
    for axis, dim in sides:
        count, length = (lax.axis_size(axis), shard.shape[dim])
        up = [(i, (i + 1) % count) for i in range(count - 1)]
        down = [(j, i) for i, j in up]
        last = lax.slice_in_dim(shard, length - width, length, axis=dim)
        initial = lax.slice_in_dim(shard, 0, width, axis=dim)
        before = lax.ppermute(last, axis, up)
        after = lax.ppermute(initial, axis, down)
        shard = jnp.concatenate([before, shard, after], axis=dim)
    return shard


def neighbours(vec):
    return extended_2(vec, (("rows", 0),), CC)


def mat_apply(mats, ext):
    flat = mats.reshape(mats.shape[0] * mats.shape[1], mats.shape[2])
    out = jnp.dot(flat, ext.reshape(ext.shape[0] * ext.shape[1]), precision=lax.Precision.HIGHEST)
    return out.reshape(mats.shape[0], mats.shape[1])


def on_device(a_tiles, a_cols, a_count, send_lists, ghost_cols, cmap, p_tiles, x_start, coarse_rhs):
    sendbuf = jnp.take(p_tiles, send_lists[0], axis=0)
    extended = extended_2(sendbuf, ((("rows", "grp"), 0),), G)
    p_ext = jnp.concatenate([p_tiles, extended[:G], extended[3 * G :]], axis=0)
    picked = jnp.take(p_ext, a_cols, axis=0)
    prod = jnp.einsum(
        "ismn,isnl->isml", a_tiles, picked, preferred_element_type=jnp.float32
    ).astype(jnp.bfloat16)
    tiles = jnp.einsum("imk,isml->iskl", p_tiles, prod, preferred_element_type=jnp.float32)
    live = (jnp.arange(K, dtype=jnp.int32)[None, :] < a_count[0][:, None]).astype(jnp.float32)
    col_map = jnp.concatenate([CC + cmap, ghost_cols[0]])
    col_block = jnp.take(col_map, a_cols, axis=0)
    row_hot = (cmap[:, None] == jnp.arange(CC, dtype=jnp.int32)[None, :]).astype(jnp.float32)
    col_hot = (col_block[:, :, None] == jnp.arange(3 * CC, dtype=jnp.int32)[None, None, :]).astype(
        jnp.float32
    ) * live[:, :, None]
    weights = row_hot[:, None, :, None] * col_hot[:, :, None, :]
    partial_value = jnp.einsum("isIJ,iskl->IkJl", weights, tiles, precision=lax.Precision.HIGHEST)
    partial_value = partial_value.reshape(CC, B, 3 * CC * B)
    theta = 13.0
    delta = 11.0
    sigma = theta / delta
    rho_zero = 1.0 / sigma
    rho_one = 1.0 / (2.0 * sigma - rho_zero)
    owned = lax.psum_scatter(partial_value, "grp", scatter_dimension=0, tiled=True)

    def apply(vec):
        whole = lax.all_gather(vec, "grp", axis=0, tiled=True)
        return mat_apply(owned, neighbours(whole))

    resid = coarse_rhs - apply(x_start)
    step_zero = resid / theta
    first_x = x_start + step_zero
    resid = resid - apply(step_zero)
    step_one = rho_one * rho_zero * step_zero + 2.0 * rho_one / delta * resid
    return (owned, first_x + step_one)


def solution(mesh):
    in_specs = (
        P(("rows", "grp"), None, None, None),
        P(("rows", "grp"), None),
        P(("rows", "grp"), None),
        P(("rows", "grp"), None),
        P(("rows", "grp"), None),
        P(("rows", "grp")),
        P(("rows", "grp"), None, None),
        P(("rows", "grp"), None),
        P(("rows", "grp"), None),
    )
    out_specs = (P(("rows", "grp"), None, None), P(("rows", "grp"), None))
    return jax.shard_map(
        on_device, mesh=mesh, in_specs=in_specs, out_specs=out_specs, check_vma=False
    )
```

profile of v0, /device:TPU:7, one launch (start us, length us, event | category | flops | bytes accessed | tf_op | source)
XLA Modules:
  0.0 109.5 jit_solution(8587857203192421967)
XLA Ops:
  7.2 0.0 copy-start
  7.2 0.0 copy-start.1
  7.2 0.0 copy-start.5
  7.2 0.0 copy-start.4
  7.2 0.0 reduce-scatter.2.cloned.1.call-start
  7.3 0.7 fusion.29
  7.9 0.7 compare_and_fusion.1
  8.6 1.5 %gather_fusion = bf16[8,128,128]{2,1,0:T(8,128)(2,1)S(1)} fusion(bf16[8,128,128]{2,1,0:T(8,128)(2,1)} %param.15, s32[1024]{0:T(1024)S(1)} %pad_clamp_fusion.1), kind=kCustom, calls=%fused_computation | custom fusion | bytes 524320 | tf_op jit(solution)/shard_map/jit(_take)/gather | solution.py:36
  10.2 0.1 broadcast_select_fusion
  10.3 4.6 %collective-permute-start = (bf16[4,128,128]{2,1,0:T(8,128)(2,1)S(1)}, bf16[4,128,128]{2,1,0:T(8,128)(2,1)S(1)}, u32[]{:S(2)}, u32[]{:S(2)}) collective-permute-start(bf16[4,128,128]{2,1,0:T(8,128)(2,1)S(1)} %get-tuple-element.8), channel_id=1, source_target_pairs={{0,1},{1,2},{2,3},{3,4},{4,5},{5,6},{6,7},{7,8},{8,9},{9,10},{10,1... | collective-permute-start | bytes 393224 | tf_op jit(solution)/shard_map/ppermute | solution.py:19
  14.8 1.9 %collective-permute-start.1 = (bf16[4,128,128]{2,1,0:T(8,128)(2,1)S(1)}, bf16[4,128,128]{2,1,0:T(8,128)(2,1)S(1)}, u32[]{:S(2)}, u32[]{:S(2)}) collective-permute-start(bf16[4,128,128]{2,1,0:T(8,128)(2,1)S(1)} %get-tuple-element.9), channel_id=1, source_target_pairs={{1,0},{2,1},{3,2},{4,3},{5,4},{6,5},{7,6},{8,7},{9,8},{10,9},{11,1... | collective-permute-start | bytes 393224 | tf_op jit(solution)/shard_map/ppermute | solution.py:20
  16.8 0.7 compare_select_fusion
  17.5 0.1 reshape.131
  17.6 0.7 broadcast_add_fusion
  18.2 0.7 pad_add_fusion
  18.9 1.2 %gather_fusion.2 = s32[120]{0:T(128)S(1)} fusion(s32[16]{0:T(128)S(1)} %pad_add_fusion, s32[1024]{0:T(1024)S(1)} %pad_clamp_fusion), kind=kCustom, calls=%fused_computation.2 | custom fusion | bytes 1440 | tf_op jit(solution)/shard_map/jit(_take)/gather | solution.py:46
  20.2 0.1 reshape.138
  20.3 0.0 copy-done.1
  20.3 0.0 copy-done.4
  20.3 0.1 fusion.28
  20.4 0.0 copy-done.5
  20.4 0.0 collective-permute-done
  20.4 0.7 collective-permute-done.1
  21.1 0.0 copy-done
  21.1 0.1 pad_maximum_fusion
  21.2 2.9 %gather_fusion.1 = bf16[120,128,128]{2,1,0:T(8,128)(2,1)} fusion(bf16[16,128,128]{2,1,0:T(8,128)(2,1)S(1)} %pad_maximum_fusion, s32[1024]{0:T(1024)S(1)} %pad_clamp_fusion), kind=kCustom, calls=%fused_computation.1 | custom fusion | bytes 7864800 | tf_op jit(solution)/shard_map/jit(_take)/gather | solution.py:39
  24.1 6.3 %copy.14 = bf16[8,15,128,128]{2,3,1,0:T(8,128)(2,1)} copy(bf16[8,15,128,128]{3,2,1,0:T(8,128)(2,1)} %bitcast.52) | data formatting | bytes 7864320 | tf_op jit(solution)/shard_map/jit(_take)/gather | solution.py:39
  30.4 10.3 %fusion.10 = f32[8,15,128,128,1]{2,3,1,0,4:T(8,128)} fusion(bf16[8,15,128,128]{3,2,1,0:T(8,128)(2,1)} %param.9, bf16[8,15,128,128]{2,3,1,0:T(8,128)(2,1)} %copy.14, pred[8,15]{1,0:T(8,128)(4,1)S(1)} %get-tuple-element.7, bf16[8,128,128]{2,1,0:T(8,128)(2,1)S(1)} %copy-done), kind=kOutput, calls=%fused_computation.9 | convolution fusion | flops 1010565120 | bytes 15990904 | tf_op jit(solution)/shard_map/imk,isml->iskl/dot_general | solution.py:43
  40.8 9.1 %copy.19 = f32[8,15,128,128,1]{3,1,0,4,2:T(8,128)} copy(f32[8,15,128,128,1]{2,3,1,0,4:T(8,128)} %fusion.10) | data formatting | bytes 15728640 | tf_op jit(solution)/shard_map/imk,isml->iskl/transpose | solution.py:43
  49.9 0.0 copy-start.3
  49.9 0.0 copy-start.2
  49.9 7.6 %convolution_bitcast_fusion = f32[2,128,6,128]{3,2,0,1:T(8,128)S(1)} fusion(f32[8,15,128,128,1]{3,1,0,4,2:T(8,128)} %copy.19, f32[8,15,6]{1,2,0:T(8,128)S(1)} %fusion.27, f32[8,2]{0,1:T(2,128)S(1)} %compare_convert_fusion), kind=kOutput, calls=%fused_computation.11 | convolution fusion | flops 283116960 | bytes 8653696 | tf_op jit(solution)/shard_map/isIJ,iskl->IkJl/dot_general | solution.py:52
  57.5 1.3 %copy.16 = f32[2,128,6,128]{1,3,2,0:T(8,128)} copy(f32[2,128,6,128]{3,2,0,1:T(8,128)S(1)} %convolution_bitcast_fusion) | data formatting | bytes 1572864 | tf_op jit(solution)/shard_map/isIJ,iskl->IkJl/transpose | solution.py:52
  58.8 0.0 reduce-scatter.2.cloned.1.call-update
  58.8 0.0 copy-done.3
  58.8 14.1 %all-gather = f32[2,1,128]{2,1,0:T(1,128)S(1)} all-gather(f32[1,1,128]{2,1,0:T(1,128)S(1)} %bitcast.60), channel_id=1, replica_groups=mesh['rows'=384,'grp'=2] {'grp'}, dimensions={0}, use_global_device_ids=true | all-gather | bytes 1536 | tf_op jit(solution)/shard_map/all_gather | solution.py:62
  72.9 1.9 %collective-permute-start.2 = (f32[2,128]{1,0:T(2,128)S(1)}, f32[2,128]{1,0:T(2,128)S(1)}, u32[]{:S(2)}, u32[]{:S(2)}) collective-permute-start(f32[2,128]{1,0:T(2,128)S(1)} %bitcast.57), channel_id=1, source_target_pairs={{0,2},{2,4},{4,6},{6,8},{8,10},{10,12},{12,14},{14,16},{16,18},{18... | collective-permute-start | bytes 3080 | tf_op jit(solution)/shard_map/ppermute | solution.py:19
  74.8 7.6 %collective-permute-start.3 = (f32[2,128]{1,0:T(2,128)S(1)}, f32[2,128]{1,0:T(2,128)S(1)}, u32[]{:S(2)}, u32[]{:S(2)}) collective-permute-start(f32[2,128]{1,0:T(2,128)S(1)} %bitcast.58), channel_id=1, source_target_pairs={{2,0},{4,2},{6,4},{8,6},{10,8},{12,10},{14,12},{16,14},{18,16},{20... | collective-permute-start | bytes 3080 | tf_op jit(solution)/shard_map/ppermute | solution.py:20
  82.4 0.0 collective-permute-done.2
  82.4 0.7 collective-permute-done.3
  83.1 1.9 %reduce-scatter.2.cloned.1.call-done = f32[1,128,768]{1,2,0:T(8,128)} async-done(((f32[2,128,768]{1,2,0:T(8,128)}), f32[1,128,768]{1,2,0:T(8,128)}) %reduce-scatter.2.cloned.1.call-update) | async-done | bytes 393232 | tf_op jit(solution)/shard_map/reduce_scatter | solution.py:59
  85.0 0.0 copy-done.2
  85.0 1.3 %convolution_subtract_fusion.1 = f32[1,128]{1,0:T(1,128)S(1)} fusion(f32[1,128]{1,0:T(1,128)S(1)} %copy-done.2, f32[768,1]{0,1:T(1,128)S(1)} %reshape.157, f32[1,128,768]{1,2,0:T(8,128)} %reduce-scatter.2.cloned.1.call-done), kind=kOutput, calls=%fused_computation.13 | convolution fusion | flops 1179776 | bytes 397312 | tf_op jit(solution)/shard_map/dot_general | solution.py:31
  86.3 1.8 %all-gather.1 = f32[2,1,128]{2,1,0:T(1,128)S(1)} all-gather(f32[1,1,128]{2,1,0:T(1,128)S(1)} %multiply_bitcast_fusion), channel_id=1, replica_groups=mesh['rows'=384,'grp'=2] {'grp'}, dimensions={0}, use_global_device_ids=true | all-gather | bytes 1536 | tf_op jit(solution)/shard_map/all_gather | solution.py:62
  88.1 3.3 %collective-permute-start.4 = (f32[2,128]{1,0:T(2,128)S(1)}, f32[2,128]{1,0:T(2,128)S(1)}, u32[]{:S(2)}, u32[]{:S(2)}) collective-permute-start(f32[2,128]{1,0:T(2,128)S(1)} %bitcast.54), channel_id=1, source_target_pairs={{0,2},{2,4},{4,6},{6,8},{8,10},{10,12},{12,14},{14,16},{16,18},{18... | collective-permute-start | bytes 3080 | tf_op jit(solution)/shard_map/ppermute | solution.py:19
  91.3 7.5 %collective-permute-start.5 = (f32[2,128]{1,0:T(2,128)S(1)}, f32[2,128]{1,0:T(2,128)S(1)}, u32[]{:S(2)}, u32[]{:S(2)}) collective-permute-start(f32[2,128]{1,0:T(2,128)S(1)} %bitcast.55), channel_id=1, source_target_pairs={{2,0},{4,2},{6,4},{8,6},{10,8},{12,10},{14,12},{16,14},{18,16},{20... | collective-permute-start | bytes 3080 | tf_op jit(solution)/shard_map/ppermute | solution.py:20
  98.8 1.9 %copy.17 = f32[1,128,768]{2,1,0:T(8,128)} copy(f32[1,128,768]{1,2,0:T(8,128)} %reduce-scatter.2.cloned.1.call-done) | data formatting | bytes 786432
  100.8 0.0 collective-permute-done.4
  100.8 0.0 collective-permute-done.5
  100.8 1.8 %fusion.19 = f32[1,128]{1,0:T(1,128)} fusion(f32[1,128]{1,0:T(1,128)S(1)} %convolution_subtract_fusion.1, f32[768,1]{0,1:T(1,128)S(1)} %reshape.159, f32[1,128,768]{1,2,0:T(8,128)} %reduce-scatter.2.cloned.1.call-done, f32[1,128]{1,0:T(1,128)S(1)} %copy-done.3), kind=kOutput, calls=%fused_computation.16 | convolution fusion | flops 1180544 | bytes 397824 | tf_op jit(solution)/shard_map/dot_general | solution.py:31
  (11 shorter events, 0.1 us)
Async XLA Ops:
  7.2 14.0 %copy-start = (bf16[8,128,128]{2,1,0:T(8,128)(2,1)S(1)}, bf16[8,128,128]{2,1,0:T(8,128)(2,1)}, u32[]{:S(2)}) copy-start(bf16[8,128,128]{2,1,0:T(8,128)(2,1)} %param.15) | copy-start | bytes 786436
  7.2 13.1 %copy-start.1 = (s32[8,15]{1,0:T(8,128)S(1)}, s32[8,15]{1,0:T(8,128)}, u32[]{:S(2)}) copy-start(s32[8,15]{1,0:T(8,128)} %param.10) | copy-start | bytes 1444
  7.2 13.2 %copy-start.5 = (s32[8]{0:T(128)S(1)}, s32[8]{0:T(128)}, u32[]{:S(2)}) copy-start(s32[8]{0:T(128)} %param.14) | copy-start | bytes 100
  7.2 13.1 %copy-start.4 = (s32[1,8]{1,0:T(1,128)S(1)}, s32[1,8]{1,0:T(1,128)}, u32[]{:S(2)}) copy-start(s32[1,8]{1,0:T(1,128)} %param.11) | copy-start | bytes 100
  7.2 77.8 %reduce-scatter.2.cloned.1.call-start = ((), (), s32[]{:S(2)}) async-start(), calls=%async_computation.1 | async-start | bytes 1179648 | tf_op jit(solution)/shard_map/reduce_scatter | solution.py:59
  10.3 10.1 %collective-permute-start = (bf16[4,128,128]{2,1,0:T(8,128)(2,1)S(1)}, bf16[4,128,128]{2,1,0:T(8,128)(2,1)S(1)}, u32[]{:S(2)}, u32[]{:S(2)}) collective-permute-start(bf16[4,128,128]{2,1,0:T(8,128)(2,1)S(1)} %get-tuple-element.8), channel_id=1, source_target_pairs={{0,1},{1,2},{2,3},{3,4},{4,5},{5,6},{6,7},{7,8},{8,9},{9,10},{10,1... | collective-permute-start | bytes 393224 | tf_op jit(solution)/shard_map/ppermute | solution.py:19
  14.8 6.3 %collective-permute-start.1 = (bf16[4,128,128]{2,1,0:T(8,128)(2,1)S(1)}, bf16[4,128,128]{2,1,0:T(8,128)(2,1)S(1)}, u32[]{:S(2)}, u32[]{:S(2)}) collective-permute-start(bf16[4,128,128]{2,1,0:T(8,128)(2,1)S(1)} %get-tuple-element.9), channel_id=1, source_target_pairs={{1,0},{2,1},{3,2},{4,3},{5,4},{6,5},{7,6},{8,7},{9,8},{10,9},{11,1... | collective-permute-start | bytes 393224 | tf_op jit(solution)/shard_map/ppermute | solution.py:20
  49.9 8.9 %copy-start.3 = (f32[1,128]{1,0:T(1,128)S(1)}, f32[1,128]{1,0:T(1,128)}, u32[]{:S(2)}) copy-start(f32[1,128]{1,0:T(1,128)} %param.16) | copy-start | bytes 1540
  49.9 35.1 %copy-start.2 = (f32[1,128]{1,0:T(1,128)S(1)}, f32[1,128]{1,0:T(1,128)}, u32[]{:S(2)}) copy-start(f32[1,128]{1,0:T(1,128)} %param.17) | copy-start | bytes 1540
  72.9 9.5 %collective-permute-start.2 = (f32[2,128]{1,0:T(2,128)S(1)}, f32[2,128]{1,0:T(2,128)S(1)}, u32[]{:S(2)}, u32[]{:S(2)}) collective-permute-start(f32[2,128]{1,0:T(2,128)S(1)} %bitcast.57), channel_id=1, source_target_pairs={{0,2},{2,4},{4,6},{6,8},{8,10},{10,12},{12,14},{14,16},{16,18},{18... | collective-permute-start | bytes 3080 | tf_op jit(solution)/shard_map/ppermute | solution.py:19
  74.8 8.3 %collective-permute-start.3 = (f32[2,128]{1,0:T(2,128)S(1)}, f32[2,128]{1,0:T(2,128)S(1)}, u32[]{:S(2)}, u32[]{:S(2)}) collective-permute-start(f32[2,128]{1,0:T(2,128)S(1)} %bitcast.58), channel_id=1, source_target_pairs={{2,0},{4,2},{6,4},{8,6},{10,8},{12,10},{14,12},{16,14},{18,16},{20... | collective-permute-start | bytes 3080 | tf_op jit(solution)/shard_map/ppermute | solution.py:20
  88.1 12.7 %collective-permute-start.4 = (f32[2,128]{1,0:T(2,128)S(1)}, f32[2,128]{1,0:T(2,128)S(1)}, u32[]{:S(2)}, u32[]{:S(2)}) collective-permute-start(f32[2,128]{1,0:T(2,128)S(1)} %bitcast.54), channel_id=1, source_target_pairs={{0,2},{2,4},{4,6},{6,8},{8,10},{10,12},{12,14},{14,16},{16,18},{18... | collective-permute-start | bytes 3080 | tf_op jit(solution)/shard_map/ppermute | solution.py:19
  91.3 9.4 %collective-permute-start.5 = (f32[2,128]{1,0:T(2,128)S(1)}, f32[2,128]{1,0:T(2,128)S(1)}, u32[]{:S(2)}, u32[]{:S(2)}) collective-permute-start(f32[2,128]{1,0:T(2,128)S(1)} %bitcast.55), channel_id=1, source_target_pairs={{2,0},{4,2},{6,4},{8,6},{10,8},{12,10},{14,12},{16,14},{18,16},{20... | collective-permute-start | bytes 3080 | tf_op jit(solution)/shard_map/ppermute | solution.py:20
Sparse Core Ops, SparseCore 0:
  58.9 26.0 reduce-scatter.1
where the time goes:
time: 110 us; the launch traced here: 109 us
  starting transfers between devices  26.8 us (24%)
  local copies, waits for them, and re-layouts  24.5 us (22%)
  matrix products  21.1 us (19%)
  blocking collectives  15.8 us (14%)
  between operations  14.2 us (13%)
  other arithmetic  3.7 us (3%)
  waiting for transfers between devices  3.34 us (3%)
    ppermute x3, starting transfers between devices, extended_2(): after = lax.ppermute(initial, axis, down)  17 us
    all_gather x2, blocking collectives, apply(): whole = lax.all_gather(vec, 'grp', axis=0, tiled=True)  15.8 us
    dot_general x1, matrix products, on_device(): jnp.einsum('imk,isml->iskl', p_tiles, prod, preferred_element_type=jnp.fl...  10.3 us
    ppermute x3, starting transfers between devices, extended_2(): before = lax.ppermute(last, axis, up)  9.72 us
    gather x2, local copies, waits for them, and re-layouts, on_device(): picked = jnp.take(p_ext, a_cols, axis=0)  9.23 us
    transpose x1, local copies, waits for them, and re-layouts, on_device(): jnp.einsum('imk,isml->iskl', p_tiles, prod, preferred_element_type=jnp.fl...  9.14 us
    dot_general x1, matrix products, on_device(): jnp.einsum('isIJ,iskl->IkJl', weights, tiles, precision=lax.Precision.HIG...  7.61 us
    dot_general x2, matrix products, mat_apply(): jnp.dot(flat, ext.reshape(ext.shape[0] * ext.shape[1]), precision=lax.Pre...  3.14 us
  transfers between devices with their start and end apart: 7, of which 3 were waited for; matrix products, arithmetic and copies ran while one was open for 5% of the time, Pallas kernels for 0%

commit v1 on v0

v1 whole, which is shorter than its diff:
```python
import jax
import jax.numpy as jnp
from jax import lax
from jax.experimental import pallas as pl
from jax.experimental.pallas import tpu as pltpu
from jax.sharding import PartitionSpec as P

B = 128
RB = 8
K = 15
G = 4
CC = 2
NJ = 3 * CC
NLIVE = 40
VECS = 16
MSG = 8 * B + 8

THETA = 13.0
DELTA = 11.0
SIGMA = THETA / DELTA
RHO0 = 1.0 / SIGMA
RHO1 = 1.0 / (2.0 * SIGMA - RHO0)

F32 = jnp.float32
BF16 = jnp.bfloat16
AXES = ("rows", "grp")
HBM = pl.BlockSpec(memory_space=pltpu.HBM)
VMEM = pl.BlockSpec(memory_space=pltpu.VMEM)
DMA = pltpu.SemaphoreType.DMA


def split3(x):
    hi = x.astype(BF16).astype(F32)
    mid = (x - hi).astype(BF16).astype(F32)
    return [hi, mid, x - hi - mid]


def padded(parts):
    rows = sum(part.shape[0] for part in parts)
    return jnp.concatenate(parts + [jnp.zeros((VECS - rows, B), F32)], axis=0).astype(BF16)


def matvec(blocks, vecs):
    acc = blocks[0] * vecs[0]
    for blk, vec in zip(blocks[1:], vecs[1:]):
        acc = acc + blk * vec
    return jnp.sum(acc.T, axis=0, keepdims=True)


def pack_kernel(send, p, x, out_a, out_b, p_out, send_s, x_v, sems):
    g = lax.axis_index("grp")
    copies = [
        pltpu.make_async_copy(send, send_s, sems.at[0]),
        pltpu.make_async_copy(p, p_out, sems.at[1]),
        pltpu.make_async_copy(x, x_v, sems.at[2]),
    ]
    for copy in copies:
        copy.start()
    for copy in copies:
        copy.wait()
    for k in range(G):
        out_a[k * B : (k + 1) * B, :] = p_out[send_s[0, G * (1 - g) + k]]
        out_b[k * B : (k + 1) * B, :] = p_out[send_s[0, G * g + k]]
    out_a[G * B :, :] = padded(split3(x_v[...]))


def pair_kernel(got_a, b_in, out_b, x_out):
    rows = [got_a[c, G * B :, :].astype(F32) for c in range(CC)]
    terms = [jnp.concatenate([r[k : k + 1] for r in rows], axis=0) for k in range(3)]
    out_b[: G * B, :] = b_in[: G * B, :]
    out_b[G * B :, :] = padded(terms)
    x_out[...] = terms[0] + terms[1] + terms[2]


def coarse_kernel(cols, count, ghost, cmap, a, p, got_a, mh, mg, tb, t, pt, cols_s, count_s, ghost_s, cmap_s, sems):
    g = lax.axis_index("grp")
    h = 1 - g
    copies = [
        pltpu.make_async_copy(src, dst, sems.at[n])
        for n, (src, dst) in enumerate([(cols, cols_s), (count, count_s), (ghost, ghost_s), (cmap, cmap_s)])
    ]
    for copy in copies:
        copy.start()
    t[...] = jnp.zeros_like(t)
    mh[...] = jnp.zeros_like(mh)
    mg[...] = jnp.zeros_like(mg)
    for i in range(RB):
        pt[i] = p[i].T
    for copy in copies:
        copy.wait()
    i = jnp.int32(0)
    s = jnp.int32(0)
    for n in range(NLIVE):
        r = jnp.where(cmap_s[i] == g, 1, 0)
        t[cols_s[i, s], r] += jnp.dot(pt[i], a[i, s], preferred_element_type=F32)
        if n + 1 < NLIVE:
            over = s + 1 >= count_s[0, i]
            s = jnp.where(over, 0, s + 1)
            i = jnp.where(over, i + 1, i)

    def halves(c):
        tc = t[c].reshape(CC * B, B)
        hi = tc.astype(BF16)
        lo = (tc - hi.astype(F32)).astype(BF16)
        return jnp.concatenate([hi, lo], axis=1)

    def add(j, lhs, tile):
        out = jnp.dot(lhs, jnp.concatenate([tile, tile], axis=0), preferred_element_type=F32)
        mh[pl.ds(pl.multiple_of(j * B, B), B), :] += out[:B]
        mg[j] += out[B:]

    for c in range(RB):
        add(CC + cmap_s[c], halves(c), p[c])
    for k in range(G):
        q = G * h + k
        add(ghost_s[0, q], halves(RB + q), got_a[h, k * B : (k + 1) * B, :])
    for k in range(G):
        tb[k] = halves(RB + G * g + k)


def message_kernel(ghost, mh_in, mg_in, tb, recv, x, rhs, mh, mg, vec, ghost_s, sems):
    g = lax.axis_index("grp")
    h = 1 - g
    copy = pltpu.make_async_copy(ghost, ghost_s, sems.at[0])
    copy.start()
    mh[: NJ * B, :] = mh_in[...]
    mg[...] = mg_in[...]
    rows = recv[G * B :, :].astype(F32)
    side = rows[0:2] + rows[2:4] + rows[4:6]
    outs = []
    for k in range(G):
        tile = recv[k * B : (k + 1) * B, :]
        outs.append(jnp.dot(tb[k], jnp.concatenate([tile, tile], axis=0), preferred_element_type=F32))
    copy.wait()
    for k in range(G):
        j = ghost_s[0, G * g + k]
        mh[pl.ds(pl.multiple_of(j * B, B), B), :] += outs[k][:B]
        mg[j] += outs[k][B:]
    xs = [x[0:1, :], x[1:2, :], side[0:1], side[1:2]]
    js = [2, 3, 4 * g, 4 * g + 1]
    known_h = matvec([mh[pl.ds(pl.multiple_of(j * B, B), B), :] for j in js], xs)
    known_g = matvec([mg[j] for j in js], xs)
    for q in range(CC):
        mh[(NJ + q) * B : (NJ + q + 1) * B, :] = mg[4 * h + q]
    mh[8 * B :, :] = jnp.concatenate([rhs[...] - known_g, side, jnp.zeros((5, B), F32)], axis=0)
    vec[...] = jnp.concatenate([known_h, side, jnp.zeros((5, B), F32)], axis=0)


def step_kernel(mh, mg, msg, vec, x, rhs, mats, step, base):
    g = lax.axis_index("grp")
    h = 1 - g
    first = g == 0
    far = [msg[8 * B + 1 : 8 * B + 2, :], msg[8 * B + 2 : 8 * B + 3, :]]
    near = [vec[1:2, :], vec[2:3, :]]
    low = [jnp.where(first, n, f) for n, f in zip(near, far)]
    high = [jnp.where(first, f, n) for n, f in zip(near, far)]
    xs = low + [x[0:1, :], x[1:2, :]] + high
    blocks = []
    for j in range(NJ):
        blk = mg[j] + msg[j * B : (j + 1) * B, :]
        mats[j] = blk
        blocks.append(blk)
    resid = rhs[...] - matvec(blocks, xs)
    other = [mh[pl.ds(pl.multiple_of((4 * h + q) * B, B), B), :] for q in range(CC)]
    other += [msg[6 * B : 7 * B, :], msg[7 * B : 8 * B, :]]
    resid_h = msg[8 * B : 8 * B + 1, :] - vec[0:1, :] - matvec(other, far + near)
    d_g = resid / THETA
    d_h = resid_h / THETA
    d0 = jnp.where(first, d_g, d_h)
    d1 = jnp.where(first, d_h, d_g)
    step[...] = jnp.concatenate([d0, d1], axis=0)
    resid = resid - matvec(blocks[2:4], [d0, d1])
    x_own = jnp.where(first, x[0:1, :], x[1:2, :])
    base[...] = x_own + d_g + RHO1 * RHO0 * d_g + (2.0 * RHO1 / DELTA) * resid


def out_kernel(mats, op, sems):
    copies = [
        pltpu.make_async_copy(mats.at[j], op.at[0, :, pl.ds(j * B, B)], sems.at[j]) for j in range(NJ)
    ]
    for copy in copies:
        copy.start()
    for copy in copies:
        copy.wait()


def last_kernel(mats, ext, base, sol):
    blocks = [mats[j] for j in (0, 1, 4, 5)]
    sol[...] = base[...] - (2.0 * RHO1 / DELTA) * matvec(blocks, [ext[i : i + 1, :] for i in range(4)])


def call(kernel, out_shape, in_specs, scratch=(), out_specs=None, us=1, **kw):
    return pl.pallas_call(
        kernel,
        out_shape=out_shape,
        in_specs=in_specs,
        out_specs=out_specs or [VMEM] * len(out_shape),
        scratch_shapes=list(scratch),
        compiler_params=pltpu.CompilerParams(vmem_limit_bytes=16 << 20),
        cost_estimate=pl.CostEstimate(flops=us * 10**9, bytes_accessed=0, transcendentals=0),
        **kw,
    )


def shaped(*shape, dtype=F32):
    return jax.ShapeDtypeStruct(shape, dtype)


def ints(*shape):
    return pltpu.SMEM(shape, jnp.int32)


def on_device(a_tiles, a_cols, a_count, send_lists, ghost_cols, cmap, p_tiles, x_start, coarse_rhs):
    rows = lax.axis_size("rows")
    across, swap = [], []
    for c in range(rows):
        swap += [(2 * c, 2 * c + 1), (2 * c + 1, 2 * c)]
        if c + 1 < rows:
            across += [(2 * c + 1, 2 * c + 2), (2 * c + 2, 2 * c + 1)]

    send_a, send_b, p = call(
        pack_kernel,
        [shaped(G * B + VECS, B, dtype=BF16), shaped(G * B + VECS, B, dtype=BF16), shaped(RB, B, B, dtype=BF16)],
        [HBM] * 3,
        [ints(1, 8), pltpu.VMEM((1, B), F32), DMA((3,))],
    )(send_lists, p_tiles, x_start)
    got_a = lax.all_gather(send_a, "grp", axis=0)
    send_b, x = call(
        pair_kernel,
        [shaped(G * B + VECS, B, dtype=BF16), shaped(CC, B)],
        [VMEM] * 2,
    )(got_a, send_b)
    recv_b = lax.ppermute(send_b, AXES, across)
    mh, mg, tb = call(
        coarse_kernel,
        [shaped(NJ * B, B), shaped(NJ, B, B), shaped(G, CC * B, 2 * B, dtype=BF16)],
        [HBM] * 4 + [VMEM] * 3,
        [
            pltpu.VMEM((RB + 2 * G, CC, B, B), F32),
            pltpu.VMEM((RB, B, B), BF16),
            ints(8, 15),
            ints(1, 8),
            ints(1, 8),
            ints(8),
            DMA((4,)),
        ],
    )(a_cols, a_count, ghost_cols, cmap, a_tiles, p, got_a)
    mh, mg, vec = call(
        message_kernel,
        [shaped(MSG, B), shaped(NJ, B, B), shaped(8, B)],
        [HBM] + [VMEM] * 6,
        [ints(1, 8), DMA((1,))],
    )(ghost_cols, mh, mg, tb, recv_b, x, coarse_rhs)
    msg = lax.ppermute(mh, AXES, swap)
    mats, step, base = call(
        step_kernel,
        [shaped(NJ, B, B), shaped(CC, B), shaped(1, B)],
        [VMEM] * 6,
    )(mh, mg, msg, vec, x, coarse_rhs)
    beyond = lax.ppermute(step, AXES, across)
    (op,) = call(
        out_kernel, [shaped(1, B, NJ * B)], [VMEM], [DMA((NJ,))], out_specs=[HBM]
    )(mats)
    ext = lax.all_gather(beyond, "grp", axis=0, tiled=True)
    (sol,) = call(last_kernel, [shaped(1, B)], [VMEM] * 3)(mats, ext, base)
    return op, sol


def solution(mesh):
    two = P(AXES, None)
    three = P(AXES, None, None)
    return jax.shard_map(
        on_device,
        mesh=mesh,
        in_specs=(P(AXES, None, None, None), two, two, two, two, P(AXES), three, two, two),
        out_specs=(three, two),
        check_vma=False,
    )
```

time: 110 us -> 43.2 us (0.39)
  local copies, waits for them, and re-layouts: 24.5 us -> 2.6 us
  matrix products: 21.1 us -> 0 us
  between operations: 14.2 us -> 0.79 us
  blocking collectives: 15.8 us -> 8.4 us
  starting transfers between devices: 26.8 us -> 21.7 us
  Pallas kernels: 0 us -> 5.07 us
  other arithmetic: 3.7 us -> 0 us
    dot_general x4 -> x0, matrix products: 21.1 us -> none  [the longest x1 10.3 us: on_device(): jnp.einsum('imk,isml->iskl', p_tiles, prod, preferred_element_type=jnp.fl...]
    gather x5 -> x0, local copies, waits for them, and re-layouts: 12.1 us -> none  [the longest x2 9.23 us: on_device(): picked = jnp.take(p_ext, a_cols, axis=0)]
    transpose x2 -> x0, local copies, waits for them, and re-layouts: 10.4 us -> none  [the longest x1 9.14 us: on_device(): jnp.einsum('imk,isml->iskl', p_tiles, prod, preferred_element_type=jnp.fl...]
    all_gather x2, blocking collectives: 15.8 us -> 8.4 us  [the longest x1 6.08 us: on_device(): ext = lax.all_gather(beyond, 'grp', axis=0, tiled=True)]
    pallas_call x0 -> x7, Pallas kernels: none -> 5.07 us  [the longest x1 1.89 us: on_device(): call(coarse_kernel, [shaped(NJ * B, B), shaped(NJ, B, B), shaped(G, CC *...]
    ppermute x6 -> x3, starting transfers between devices: 26.7 us -> 21.7 us  [the longest x1 15.5 us: on_device(): msg = lax.ppermute(mh, AXES, swap)]
    ppermute x6 -> x3, waiting for transfers between devices: 1.45 us -> 4.41 us  [the longest x1 2.16 us: on_device(): beyond = lax.ppermute(step, AXES, across)]
    reduce_scatter x1 -> x0, waiting for transfers between devices: 1.88 us -> none  [on_device(): lax.psum_scatter(partial_value, 'grp', scatter_dimension=0, tiled=True)]
  transfers between devices with their start and end apart: 7 -> 3, of which waited for: 3 -> 3; matrix products, arithmetic and copies ran while one was open for 5% -> 0% of each run, Pallas kernels for 0% -> 6%
where the time goes in v1:
time: 43.2 us; the launch traced here: 43 us
  starting transfers between devices  21.7 us (50%)
  blocking collectives  8.4 us (19%)
  Pallas kernels  5.07 us (12%)
  waiting for transfers between devices  4.41 us (10%)
  local copies, waits for them, and re-layouts  2.6 us (6%)
  between operations  0.79 us (2%)
    ppermute x1, starting transfers between devices, on_device(): msg = lax.ppermute(mh, AXES, swap)  15.5 us
    all_gather x1, blocking collectives, on_device(): ext = lax.all_gather(beyond, 'grp', axis=0, tiled=True)  6.08 us
    ppermute x1, starting transfers between devices, on_device(): recv_b = lax.ppermute(send_b, AXES, across)  4.25 us
    unnamed x18, local copies, waits for them, and re-layouts  2.6 us
    all_gather x1, blocking collectives, on_device(): got_a = lax.all_gather(send_a, 'grp', axis=0)  2.31 us
    ppermute x1, waiting for transfers between devices, on_device(): beyond = lax.ppermute(step, AXES, across)  2.16 us
    ppermute x1, starting transfers between devices, on_device(): beyond = lax.ppermute(step, AXES, across)  1.92 us
    pallas_call x1, Pallas kernels, on_device(): call(coarse_kernel, [shaped(NJ * B, B), shaped(NJ, B, B), shaped(G, CC *...  1.89 us
  transfers between devices with their start and end apart: 3, of which 3 were waited for; matrix products, arithmetic and copies ran while one was open for 0% of the time, Pallas kernels for 6%

profile of v1, /device:TPU:7, one launch (start us, length us, event | category | flops | bytes accessed | tf_op | source)
XLA Modules:
  0.0 43.0 jit_solution(12972382465793412101)
XLA Ops:
  0.6 0.0 copy-start.4
  0.6 0.0 copy-start.3
  0.7 0.0 copy-start.2
  0.7 0.0 copy-start.1
  0.7 0.0 copy-start
  0.7 0.0 copy-start.5
  0.7 1.1 %copy-done.5 = bf16[8,128,128]{2,1,0:T(8,128)(2,1)S(1)} copy-done((bf16[8,128,128]{2,1,0:T(8,128)(2,1)S(1)}, bf16[8,128,128]{2,1,0:T(8,128)(2,1)}, u32[]{:S(2)}) %copy-start.5) | copy-done | bytes 262168
  1.8 0.0 copy-start.6
  1.8 0.8 %copy-done.6 = s32[1,8]{1,0:T(1,128)S(1)} copy-done((s32[1,8]{1,0:T(1,128)S(1)}, s32[1,8]{1,0:T(1,128)}, u32[]{:S(2)}) %copy-start.6) | copy-done | bytes 56
  2.6 0.0 copy-start.7
  2.6 0.7 %copy-done.7 = f32[1,128]{1,0:T(1,128)S(1)} copy-done((f32[1,128]{1,0:T(1,128)S(1)}, f32[1,128]{1,0:T(1,128)}, u32[]{:S(2)}) %copy-start.7) | copy-done | bytes 536
  3.3 0.6 %shard_map.104 = (bf16[528,128]{1,0:T(8,128)(2,1)S(1)}, bf16[528,128]{1,0:T(8,128)(2,1)S(1)}, bf16[8,128,128]{2,1,0:T(8,128)(2,1)S(1)}) custom-call(s32[1,8]{1,0:T(1,128)S(1)} %copy-done.6, bf16[8,128,128]{2,1,0:T(8,128)(2,1)S(1)} %copy-done.5, f32[1,128]{1,0:T(1,128)S(1)} %copy-done.7), custom_call_target="tpu_custom_call" | custom-call | flops 1000000000 | tf_op jit(solution)/shard_map/pallas_call | solution.py:221
  3.9 2.3 %all-gather = bf16[1056,128]{1,0:T(8,128)(2,1)S(1)} all-gather(bf16[528,128]{1,0:T(8,128)(2,1)S(1)} %get-tuple-element.17), channel_id=2, replica_groups=mesh['rows'=384,'grp'=2] {'grp'}, dimensions={0}, use_global_device_ids=true | all-gather | bytes 405504 | tf_op jit(solution)/shard_map/all_gather | solution.py:227
  6.2 0.0 copy-start.8
  6.2 4.2 %collective-permute-start = (bf16[528,128]{1,0:T(8,128)(2,1)S(1)}, bf16[528,128]{1,0:T(8,128)(2,1)S(1)}, u32[]{:S(2)}, u32[]{:S(2)}) collective-permute-start(bf16[528,128]{1,0:T(8,128)(2,1)S(1)} %get-tuple-element.22), channel_id=1, source_target_pairs={{1,2},{2,1},{3,4},{4,3},{5,6},{6,5},{7,8},{8,7},{9,10},{10,9},{11,... | collective-permute-start | bytes 405512 | tf_op jit(solution)/shard_map/ppermute | solution.py:233
  10.5 0.0 copy-done.4
  10.5 0.0 copy-done.3
  10.5 0.0 copy-done.2
  10.5 0.0 copy-done.1
  10.5 0.0 copy-done
  10.5 1.9 %shard_map.105 = (f32[768,128]{1,0:T(8,128)S(1)}, f32[6,128,128]{2,1,0:T(8,128)S(1)}, bf16[4,256,256]{2,1,0:T(8,128)(2,1)S(1)}) custom-call(s32[8,15]{1,0:T(8,128)S(1)} %copy-done.1, s32[1,8]{1,0:T(1,128)S(1)} %copy-done.2, s32[1,8]{1,0:T(1,128)S(1)} %copy-done.4, s32[8]{0:T(128)S(1)} %copy-done.3, bf16[8,15,128,128]{3,2,1,0:T(8,128)(2,1)S(1)} %copy-done, ...), custom_call_target="tpu_custom_call" | custom-call | flops 1000000000 | tf_op jit(solution)/shard_map/pallas_call | solution.py:234
  12.4 0.7 %collective-permute-done.recv = bf16[528,128]{1,0:T(8,128)(2,1)S(1)} collective-permute-done((bf16[528,128]{1,0:T(8,128)(2,1)S(1)}, bf16[528,128]{1,0:T(8,128)(2,1)S(1)}, u32[]{:S(2)}, u32[]{:S(2)}) %collective-permute-start) | collective-permute-done | bytes 135200 | tf_op jit(solution)/shard_map/ppermute | solution.py:233
  13.1 0.0 copy-done.8
  13.1 0.9 %shard_map.107 = (f32[1032,128]{1,0:T(8,128)S(1)}, f32[6,128,128]{2,1,0:T(8,128)S(1)}, f32[8,128]{1,0:T(8,128)S(1)}) custom-call(s32[1,8]{1,0:T(1,128)S(1)} %copy-done.4, f32[768,128]{1,0:T(8,128)S(1)} %get-tuple-element.18.mh_in, f32[6,128,128]{2,1,0:T(8,128)S(1)} %get-tuple-element.19.mg_in, bf16[4,256,256]{2,1,0:T(8,128)(2,1)S(1)} %get-tuple-element.20.tb, ...), custom_call_target="tpu_custom_call" | custom-call | flops 1000000000 | tf_op jit(solution)/shard_map/pallas_call | solution.py:248
  14.0 15.5 %collective-permute-start.1 = (f32[1032,128]{1,0:T(8,128)S(1)}, f32[1032,128]{1,0:T(8,128)S(1)}, u32[]{:S(2)}, u32[]{:S(2)}) collective-permute-start(f32[1032,128]{1,0:T(8,128)S(1)} %get-tuple-element.24.mh), channel_id=1, source_target_pairs={{0,1},{1,0},{2,3},{3,2},{4,5},{5,4},{6,7},{7,6},{8,9},{9,8},{10,11... | collective-permute-start | bytes 1585160 | tf_op jit(solution)/shard_map/ppermute | solution.py:254
  29.6 1.5 %collective-permute-done.1.msg = f32[1032,128]{1,0:T(8,128)S(1)} collective-permute-done((f32[1032,128]{1,0:T(8,128)S(1)}, f32[1032,128]{1,0:T(8,128)S(1)}, u32[]{:S(2)}, u32[]{:S(2)}) %collective-permute-start.1) | collective-permute-done | bytes 528416 | tf_op jit(solution)/shard_map/ppermute | solution.py:254
  31.1 0.3 shard_map.108
  31.4 1.9 %collective-permute-start.2 = (f32[2,128]{1,0:T(2,128)S(1)}, f32[2,128]{1,0:T(2,128)S(1)}, u32[]{:S(2)}, u32[]{:S(2)}) collective-permute-start(f32[2,128]{1,0:T(2,128)S(1)} %get-tuple-element.28), channel_id=1, source_target_pairs={{1,2},{2,1},{3,4},{4,3},{5,6},{6,5},{7,8},{8,7},{9,10},{10,9},{11,... | collective-permute-start | bytes 3080 | tf_op jit(solution)/shard_map/ppermute | solution.py:260
  33.3 0.8 %shard_map.109 = f32[1,128,768]{2,1,0:T(8,128)} custom-call(f32[6,128,128]{2,1,0:T(8,128)S(1)} %get-tuple-element.27.mats), custom_call_target="tpu_custom_call" | custom-call | flops 1000000000 | tf_op jit(solution)/shard_map/pallas_call | solution.py:261
  34.1 2.2 %collective-permute-done.2 = f32[2,128]{1,0:T(2,128)S(1)} collective-permute-done((f32[2,128]{1,0:T(2,128)S(1)}, f32[2,128]{1,0:T(2,128)S(1)}, u32[]{:S(2)}, u32[]{:S(2)}) %collective-permute-start.2) | collective-permute-done | bytes 1056 | tf_op jit(solution)/shard_map/ppermute | solution.py:260
  36.3 6.1 %all-gather.1 = f32[2,2,128]{2,1,0:T(2,128)S(1)} all-gather(f32[1,2,128]{2,1,0:T(2,128)S(1)} %bitcast.6), channel_id=1, replica_groups=mesh['rows'=384,'grp'=2] {'grp'}, dimensions={0}, use_global_device_ids=true | all-gather | bytes 3072 | tf_op jit(solution)/shard_map/all_gather | solution.py:264
  42.3 0.6 %shard_map.110 = f32[1,128]{1,0:T(1,128)} custom-call(f32[6,128,128]{2,1,0:T(8,128)S(1)} %get-tuple-element.27.mats, f32[4,128]{1,0:T(4,128)S(1)} %bitcast.5, f32[1,128]{1,0:T(1,128)S(1)} %get-tuple-element.29.base), custom_call_target="tpu_custom_call" | custom-call | flops 1000000000 | tf_op jit(solution)/shard_map/pallas_call | solution.py:265
  (1 shorter events, 0.0 us)
Async XLA Ops:
  0.6 9.8 %copy-start.4 = (s32[1,8]{1,0:T(1,128)S(1)}, s32[1,8]{1,0:T(1,128)}, u32[]{:S(2)}) copy-start(s32[1,8]{1,0:T(1,128)} %ghost.3) | copy-start | bytes 100
  0.6 9.8 %copy-start.3 = (s32[8]{0:T(128)S(1)}, s32[8]{0:T(128)}, u32[]{:S(2)}) copy-start(s32[8]{0:T(128)} %cmap.1) | copy-start | bytes 100
  0.7 9.8 %copy-start.2 = (s32[1,8]{1,0:T(1,128)S(1)}, s32[1,8]{1,0:T(1,128)}, u32[]{:S(2)}) copy-start(s32[1,8]{1,0:T(1,128)} %count.1) | copy-start | bytes 100
  0.7 9.8 %copy-start.1 = (s32[8,15]{1,0:T(8,128)S(1)}, s32[8,15]{1,0:T(8,128)}, u32[]{:S(2)}) copy-start(s32[8,15]{1,0:T(8,128)} %cols.1) | copy-start | bytes 1444
  0.7 9.8 %copy-start = (bf16[8,15,128,128]{3,2,1,0:T(8,128)(2,1)S(1)}, bf16[8,15,128,128]{3,2,1,0:T(8,128)(2,1)}, u32[]{:S(2)}) copy-start(bf16[8,15,128,128]{3,2,1,0:T(8,128)(2,1)} %a.1) | copy-start | bytes 11796484
  0.7 1.1 %copy-start.5 = (bf16[8,128,128]{2,1,0:T(8,128)(2,1)S(1)}, bf16[8,128,128]{2,1,0:T(8,128)(2,1)}, u32[]{:S(2)}) copy-start(bf16[8,128,128]{2,1,0:T(8,128)(2,1)} %p.1) | copy-start | bytes 786436
  1.8 0.8 %copy-start.6 = (s32[1,8]{1,0:T(1,128)S(1)}, s32[1,8]{1,0:T(1,128)}, u32[]{:S(2)}) copy-start(s32[1,8]{1,0:T(1,128)} %send.1) | copy-start | bytes 100
  2.6 0.7 %copy-start.7 = (f32[1,128]{1,0:T(1,128)S(1)}, f32[1,128]{1,0:T(1,128)}, u32[]{:S(2)}) copy-start(f32[1,128]{1,0:T(1,128)} %x.1) | copy-start | bytes 1540
  6.2 7.0 %copy-start.8 = (f32[1,128]{1,0:T(1,128)S(1)}, f32[1,128]{1,0:T(1,128)}, u32[]{:S(2)}) copy-start(f32[1,128]{1,0:T(1,128)} %rhs.3) | copy-start | bytes 1540
  6.2 6.9 %collective-permute-start = (bf16[528,128]{1,0:T(8,128)(2,1)S(1)}, bf16[528,128]{1,0:T(8,128)(2,1)S(1)}, u32[]{:S(2)}, u32[]{:S(2)}) collective-permute-start(bf16[528,128]{1,0:T(8,128)(2,1)S(1)} %get-tuple-element.22), channel_id=1, source_target_pairs={{1,2},{2,1},{3,4},{4,3},{5,6},{6,5},{7,8},{8,7},{9,10},{10,9},{11,... | collective-permute-start | bytes 405512 | tf_op jit(solution)/shard_map/ppermute | solution.py:233
  14.0 17.1 %collective-permute-start.1 = (f32[1032,128]{1,0:T(8,128)S(1)}, f32[1032,128]{1,0:T(8,128)S(1)}, u32[]{:S(2)}, u32[]{:S(2)}) collective-permute-start(f32[1032,128]{1,0:T(8,128)S(1)} %get-tuple-element.24.mh), channel_id=1, source_target_pairs={{0,1},{1,0},{2,3},{3,2},{4,5},{5,4},{6,7},{7,6},{8,9},{9,8},{10,11... | collective-permute-start | bytes 1585160 | tf_op jit(solution)/shard_map/ppermute | solution.py:254
  31.4 4.9 %collective-permute-start.2 = (f32[2,128]{1,0:T(2,128)S(1)}, f32[2,128]{1,0:T(2,128)S(1)}, u32[]{:S(2)}, u32[]{:S(2)}) collective-permute-start(f32[2,128]{1,0:T(2,128)S(1)} %get-tuple-element.28), channel_id=1, source_target_pairs={{1,2},{2,1},{3,4},{4,3},{5,6},{6,5},{7,8},{8,7},{9,10},{10,9},{11,... | collective-permute-start | bytes 3080 | tf_op jit(solution)/shard_map/ppermute | solution.py:260

commit v2 on v1

v2 whole, which is shorter than its diff:
```python
import jax
import jax.numpy as jnp
from jax import lax
from jax.experimental import pallas as pl
from jax.experimental.pallas import tpu as pltpu
from jax.sharding import PartitionSpec as P

B = 128
RB = 8
K = 15
G = 4
CC = 2
NJ = 3 * CC
NLIVE = 40
VECS = 16
COARSE_US = 0
FIRST_US = 5
AFTER_US = 5

THETA = 13.0
DELTA = 11.0
SIGMA = THETA / DELTA
RHO0 = 1.0 / SIGMA
RHO1 = 1.0 / (2.0 * SIGMA - RHO0)

F32 = jnp.float32
BF16 = jnp.bfloat16
AXES = ("rows", "grp")
HBM = pl.BlockSpec(memory_space=pltpu.HBM)
ANY = pl.BlockSpec(memory_space=pl.ANY)
VMEM = pl.BlockSpec(memory_space=pltpu.VMEM)
DMA = pltpu.SemaphoreType.DMA


def split3(x):
    hi = x.astype(BF16).astype(F32)
    mid = (x - hi).astype(BF16).astype(F32)
    return [hi, mid, x - hi - mid]


def padded(parts):
    rows = sum(part.shape[0] for part in parts)
    return jnp.concatenate(parts + [jnp.zeros((VECS - rows, B), F32)], axis=0).astype(BF16)


def matvec(blocks, vecs):
    acc = blocks[0] * vecs[0]
    for blk, vec in zip(blocks[1:], vecs[1:]):
        acc = acc + blk * vec
    return jnp.sum(acc.T, axis=0, keepdims=True)


def first_kernel(out):
    out[...] = jnp.zeros_like(out)


def pack_kernel(zero, send, p, x, out_a, out_b, out_p):
    first = lax.axis_index("grp") == 0
    lists = send[...]
    low = [lists[0, k] for k in range(G)]
    high = [lists[0, G + k] for k in range(G)]
    out_a[G * B :, :] = padded(split3(x[...] + zero[0:1, :]))
    out_p[...] = p[...]
    for k in range(G):
        out_a[k * B : (k + 1) * B, :] = p[jnp.where(first, high[k], low[k])]
        out_b[k * B : (k + 1) * B, :] = p[jnp.where(first, low[k], high[k])]


def pair_kernel(got_a, tiles, out_b, x):
    rows = [got_a[c, G * B :, :].astype(F32) for c in range(CC)]
    terms = [jnp.concatenate([r[k : k + 1] for r in rows], axis=0) for k in range(3)]
    out_b[: G * B, :] = tiles[...]
    out_b[G * B :, :] = padded(terms)
    x[...] = terms[0] + terms[1] + terms[2]


def coarse_kernel(cols, count, ghost, cmap, a, p, got_a, mh, mg, tb, t, pt, cols_s, count_s, ghost_s, cmap_s, sems):
    g = lax.axis_index("grp")
    h = 1 - g
    copies = [
        pltpu.make_async_copy(src, dst, sems.at[n])
        for n, (src, dst) in enumerate([(cols, cols_s), (count, count_s), (ghost, ghost_s), (cmap, cmap_s)])
    ]
    for copy in copies:
        copy.start()
    t[...] = jnp.zeros_like(t)
    mh[...] = jnp.zeros_like(mh)
    mg[...] = jnp.zeros_like(mg)
    for i in range(RB):
        pt[i] = p[i].T
    for copy in copies:
        copy.wait()
    i = jnp.int32(0)
    s = jnp.int32(0)
    for n in range(NLIVE):
        r = jnp.where(cmap_s[i] == g, 1, 0)
        t[cols_s[i, s], r] += jnp.dot(pt[i], a[i, s], preferred_element_type=F32)
        if n + 1 < NLIVE:
            over = s + 1 >= count_s[0, i]
            s = jnp.where(over, 0, s + 1)
            i = jnp.where(over, i + 1, i)

    def halves(c):
        tc = t[c].reshape(CC * B, B)
        hi = tc.astype(BF16)
        lo = (tc - hi.astype(F32)).astype(BF16)
        return jnp.concatenate([hi, lo], axis=1)

    def add(j, lhs, tile):
        out = jnp.dot(lhs, jnp.concatenate([tile, tile], axis=0), preferred_element_type=F32)
        mh[j] += out[:B]
        mg[j] += out[B:]

    for c in range(RB):
        add(CC + cmap_s[c], halves(c), p[c])
    for k in range(G):
        q = G * h + k
        add(ghost_s[0, q], halves(RB + q), got_a[h, k * B : (k + 1) * B, :])
    for k in range(G):
        tb[k] = halves(RB + G * g + k)


def known(g):
    return [4 * g, 4 * g + 1]


def message_kernel(ghost, recv, mh_in, mg_in, tb, x, rhs, mh, mg, ext, vec):
    g = lax.axis_index("grp")
    first = g == 0
    lists = ghost[...]
    js = [jnp.where(first, lists[0, k], lists[0, G + k]) for k in range(G)]
    mh[...] = mh_in[...]
    mg[...] = mg_in[...]
    outs = []
    for k in range(G):
        tile = recv[k * B : (k + 1) * B, :]
        outs.append(jnp.dot(tb[k], jnp.concatenate([tile, tile], axis=0), preferred_element_type=F32))
    for k in range(G):
        j = js[k]
        mh[j] += outs[k][:B]
        mg[j] += outs[k][B:]
    rows = recv[G * B :, :].astype(F32)
    near = rows[0:2] + rows[2:4] + rows[4:6]
    xs = [x[0:1, :], x[1:2, :], near[0:1], near[1:2]]
    js = [2, 3] + known(g)
    w_h = matvec([mh[j] for j in js], xs)
    w_g = matvec([mg[j] for j in js], xs)
    for j in range(NJ):
        hi = mh[j].astype(BF16)
        ext[j * B : (j + 1) * B, :] = hi
        ext[(NJ + j) * B : (NJ + j + 1) * B, :] = (mh[j] - hi.astype(F32)).astype(BF16)
    for q, j in enumerate(known(1 - g)):
        ext[(2 * NJ + q) * B : (2 * NJ + q + 1) * B, :] = mg[j].astype(BF16)
    rows = jnp.concatenate([w_h, rhs[...] - w_g, near], axis=0)
    ext[14 * B :, :] = padded(split3(rows))
    vec[...] = rows


def wide(exts, c, j):
    return (
        exts[c, pl.ds(pl.multiple_of(j * B, B), B), :].astype(F32)
        + exts[c, pl.ds(pl.multiple_of((NJ + j) * B, B), B), :].astype(F32)
    )


def step_kernel(exts, mh, mg, vec, x, step, base):
    g = lax.axis_index("grp")
    h = 1 - g
    first = g == 0
    rows = exts[h, 14 * B :, :].astype(F32)
    far = rows[0:4] + rows[4:8] + rows[8:12]
    xs = [far[2:3], far[3:4], vec[2:3, :], vec[3:4, :]]
    in_g = [mg[j] for j in known(h)] + [wide(exts, h, j) for j in known(g)]
    in_h = [mh[j] for j in known(h)] + [exts[h, (12 + q) * B : (13 + q) * B, :].astype(F32) for q in range(CC)]
    resid = vec[1:2, :] - far[0:1] - matvec(in_g, xs)
    resid_h = far[1:2] - vec[0:1, :] - matvec(in_h, xs)
    d_g = resid / THETA
    d_h = resid_h / THETA
    step[...] = jnp.concatenate([jnp.where(first, d_g, d_h), jnp.where(first, d_h, d_g)], axis=0)
    x_own = jnp.where(first, x[0:1, :], x[1:2, :])
    base[...] = x_own + d_g + RHO1 * RHO0 * d_g + (2.0 * RHO1 / DELTA) * resid


def sum_kernel(mg, exts, step, base_in, mats, base, op, sems):
    h = 1 - lax.axis_index("grp")
    copies = []
    for j in range(NJ):
        mats[j] = mg[j] + wide(exts, h, j)
        copies.append(pltpu.make_async_copy(mats.at[j], op.at[0, :, pl.ds(j * B, B)], sems.at[j]))
        copies[-1].start()
    own = matvec([mats[2], mats[3]], [step[0:1, :], step[1:2, :]])
    base[...] = base_in[...] - (2.0 * RHO1 / DELTA) * own
    for copy in copies:
        copy.wait()


def last_kernel(mats, ext, base, sol):
    blocks = [mats[j] for j in (0, 1, 4, 5)]
    sol[...] = base[...] - (2.0 * RHO1 / DELTA) * matvec(blocks, [ext[i : i + 1, :] for i in range(4)])


def call(kernel, out_shape, in_specs, scratch=(), out_specs=None, us=1, vm=16, **kw):
    return pl.pallas_call(
        kernel,
        out_shape=out_shape,
        in_specs=in_specs,
        out_specs=out_specs or [VMEM] * len(out_shape),
        scratch_shapes=list(scratch),
        compiler_params=pltpu.CompilerParams(vmem_limit_bytes=vm << 20),
        cost_estimate=pl.CostEstimate(flops=us * 10**9, bytes_accessed=0, transcendentals=0),
        **kw,
    )


def after_kernel(*refs):
    pass


def after(value, *others):
    (out,) = call(
        after_kernel,
        [shaped(*value.shape, dtype=value.dtype)],
        [ANY] * (1 + len(others)),
        out_specs=[ANY],
        input_output_aliases={0: 0},
        us=AFTER_US,
    )(value, *others)
    return out


def shaped(*shape, dtype=F32):
    return jax.ShapeDtypeStruct(shape, dtype)


def ints(*shape):
    return pltpu.SMEM(shape, jnp.int32)


def on_device(a_tiles, a_cols, a_count, send_lists, ghost_cols, cmap, p_tiles, x_start, coarse_rhs):
    rows = lax.axis_size("rows")
    near = []
    for c in range(rows - 1):
        near += [(2 * c + 1, 2 * c + 2), (2 * c + 2, 2 * c + 1)]

    part = shaped(NJ, B, B)
    packed = shaped(G * B + VECS, B, dtype=BF16)
    (zero,) = call(first_kernel, [shaped(8, B)], [], us=FIRST_US)()
    send_a, send_b, p = call(
        pack_kernel,
        [packed, shaped(G * B, B, dtype=BF16), shaped(RB, B, B, dtype=BF16)],
        [VMEM] * 4,
    )(zero, send_lists, p_tiles, x_start)
    got_a = lax.all_gather(send_a, "grp", axis=0)
    send_b, x = call(pair_kernel, [packed, shaped(CC, B)], [VMEM] * 2)(got_a, send_b)
    recv_b = lax.ppermute(send_b, AXES, near)
    mh, mg, tb = call(
        coarse_kernel,
        [part, part, shaped(G, CC * B, 2 * B, dtype=BF16)],
        [HBM] * 4 + [VMEM] * 3,
        [
            pltpu.VMEM((RB + 2 * G, CC, B, B), F32),
            pltpu.VMEM((RB, B, B), BF16),
            ints(8, 15),
            ints(1, 8),
            ints(1, 8),
            ints(8),
            DMA((4,)),
        ],
        us=COARSE_US,
    )(a_cols, a_count, ghost_cols, cmap, a_tiles, p, got_a)
    mh, mg, ext, vec = call(
        message_kernel,
        [part, part, shaped(14 * B + VECS, B, dtype=BF16), shaped(4, B)],
        [VMEM] * 7,
    )(ghost_cols, recv_b, mh, mg, tb, x, coarse_rhs)
    exts = lax.all_gather(ext, "grp", axis=0)
    step, base = call(step_kernel, [shaped(CC, B), shaped(1, B)], [VMEM] * 5)(exts, mh, mg, vec, x)
    beyond = lax.ppermute(step, AXES, near)
    mats, base, op = call(
        sum_kernel,
        [part, shaped(1, B), shaped(1, B, NJ * B)],
        [VMEM] * 4,
        [DMA((NJ,))],
        out_specs=[VMEM, VMEM, HBM],
    )(mg, exts, step, base)
    around = lax.all_gather(after(beyond, base), "grp", axis=0, tiled=True)
    (sol,) = call(last_kernel, [shaped(1, B)], [VMEM] * 3)(mats, around, base)
    return op, sol


def solution(mesh):
    two = P(AXES, None)
    three = P(AXES, None, None)
    return jax.shard_map(
        on_device,
        mesh=mesh,
        in_specs=(P(AXES, None, None, None), two, two, two, two, P(AXES), three, two, two),
        out_specs=(three, two),
        check_vma=False,
    )
```

time: 43.2 us -> 39.3 us (0.910)
  blocking collectives: 8.4 us -> 24.2 us
  starting transfers between devices: 21.7 us -> 6.17 us
  local copies, waits for them, and re-layouts: 2.6 us -> 0.96 us
  waiting for transfers between devices: 4.41 us -> 2.85 us
  Pallas kernels: 5.07 us -> 4.15 us
    all_gather x1 -> x2, blocking collectives: 6.08 us -> 21.8 us  [the longest x1 15.7 us: on_device(): exts = lax.all_gather(ext, 'grp', axis=0)]
    ppermute x3 -> x2, starting transfers between devices: 21.7 us -> 6.17 us  [the longest x1 4.25 us: on_device(): recv_b = lax.ppermute(send_b, AXES, near)]
    unnamed x18, local copies, waits for them, and re-layouts: 2.6 us -> 0.96 us
    ppermute x3 -> x2, waiting for transfers between devices: 4.41 us -> 2.85 us  [the longest x1 2.14 us: on_device(): beyond = lax.ppermute(step, AXES, near)]
    pallas_call x7 -> x9, Pallas kernels: 5.07 us -> 4.15 us  [the longest x1 1.91 us: on_device(): call(coarse_kernel, [part, part, shaped(G, CC * B, 2 * B, dtype=BF16)], [...]
  transfers between devices with their start and end apart: 3 -> 2, of which waited for: 3 -> 2; matrix products, arithmetic and copies ran while one was open for 0% -> 0% of each run, Pallas kernels for 6% -> 7%
where the time goes in v2:
time: 39.3 us; the launch traced here: 39.2 us
  blocking collectives  24.2 us (62%)
  starting transfers between devices  6.17 us (16%)
  Pallas kernels  4.15 us (11%)
  waiting for transfers between devices  2.85 us (7%)
  local copies, waits for them, and re-layouts  0.96 us (2%)
  between operations  0.77 us (2%)
    all_gather x1, blocking collectives, on_device(): exts = lax.all_gather(ext, 'grp', axis=0)  15.7 us
    all_gather x1, blocking collectives, on_device(): around = lax.all_gather(after(beyond, base), 'grp', axis=0, tiled=True)  6.09 us
    ppermute x1, starting transfers between devices, on_device(): recv_b = lax.ppermute(send_b, AXES, near)  4.25 us
    all_gather x1, blocking collectives, on_device(): got_a = lax.all_gather(send_a, 'grp', axis=0)  2.45 us
    ppermute x1, waiting for transfers between devices, on_device(): beyond = lax.ppermute(step, AXES, near)  2.14 us
    ppermute x1, starting transfers between devices, on_device(): beyond = lax.ppermute(step, AXES, near)  1.92 us
    pallas_call x1, Pallas kernels, on_device(): call(coarse_kernel, [part, part, shaped(G, CC * B, 2 * B, dtype=BF16)], [...  1.91 us
    unnamed x18, local copies, waits for them, and re-layouts  0.96 us
  transfers between devices with their start and end apart: 2, of which 2 were waited for; matrix products, arithmetic and copies ran while one was open for 0% of the time, Pallas kernels for 7%

profile of v2, /device:TPU:7, one launch (start us, length us, event | category | flops | bytes accessed | tf_op | source)
XLA Modules:
  0.0 39.2 jit_solution(13004911219507237295)
XLA Ops:
  0.6 0.0 copy-start.7
  0.6 0.0 copy-start.5
  0.7 0.0 copy-start.6
  0.7 0.6 %copy-done.7 = f32[1,128]{1,0:T(1,128)S(1)} copy-done((f32[1,128]{1,0:T(1,128)S(1)}, f32[1,128]{1,0:T(1,128)}, u32[]{:S(2)}) %copy-start.7) | copy-done | bytes 536
  1.3 0.3 copy-done.5
  1.6 0.0 copy-done.6
  1.6 0.0 copy-start
  1.6 0.0 copy-start.1
  1.6 0.0 copy-start.2
  1.6 0.0 copy-start.3
  1.6 0.0 copy-start.4
  1.6 0.1 shard_map.105
  1.8 2.4 %all-gather = bf16[1056,128]{1,0:T(8,128)(2,1)S(1)} all-gather(bf16[528,128]{1,0:T(8,128)(2,1)S(1)} %get-tuple-element.19), channel_id=2, replica_groups=mesh['rows'=384,'grp'=2] {'grp'}, dimensions={0}, use_global_device_ids=true | all-gather | bytes 405504 | tf_op jit(solution)/shard_map/all_gather | solution.py:253
  4.2 0.0 copy-start.8
  4.2 4.2 %collective-permute-start = (bf16[528,128]{1,0:T(8,128)(2,1)S(1)}, bf16[528,128]{1,0:T(8,128)(2,1)S(1)}, u32[]{:S(2)}, u32[]{:S(2)}) collective-permute-start(bf16[528,128]{1,0:T(8,128)(2,1)S(1)} %get-tuple-element.21), channel_id=1, source_target_pairs={{1,2},{2,1},{3,4},{4,3},{5,6},{6,5},{7,8},{8,7},{9,10},{10,9},{11,... | collective-permute-start | bytes 405512 | tf_op jit(solution)/shard_map/ppermute | solution.py:255
  8.5 0.0 copy-done
  8.5 0.0 copy-done.1
  8.5 0.0 copy-done.2
  8.5 0.0 copy-done.3
  8.5 0.0 copy-done.4
  8.5 1.9 %shard_map.107 = (f32[6,128,128]{2,1,0:T(8,128)S(1)}, f32[6,128,128]{2,1,0:T(8,128)S(1)}, bf16[4,256,256]{2,1,0:T(8,128)(2,1)S(1)}) custom-call(s32[8,15]{1,0:T(8,128)S(1)} %copy-done.1, s32[1,8]{1,0:T(1,128)S(1)} %copy-done.2, s32[1,8]{1,0:T(1,128)S(1)} %copy-done.4, s32[8]{0:T(128)S(1)} %copy-done.3, bf16[8,15,128,128]{3,2,1,0:T(8,128)(2,1)S(1)} %copy-done, ...), custom_call_target="tpu_custom_call" | custom-call | tf_op jit(solution)/shard_map/pallas_call | solution.py:256
  10.5 0.7 %collective-permute-done.recv = bf16[528,128]{1,0:T(8,128)(2,1)S(1)} collective-permute-done((bf16[528,128]{1,0:T(8,128)(2,1)S(1)}, bf16[528,128]{1,0:T(8,128)(2,1)S(1)}, u32[]{:S(2)}, u32[]{:S(2)}) %collective-permute-start) | collective-permute-done | bytes 135200 | tf_op jit(solution)/shard_map/ppermute | solution.py:255
  11.2 0.0 copy-done.8
  11.2 0.5 %shard_map.108 = (f32[6,128,128]{2,1,0:T(8,128)S(1)}, f32[6,128,128]{2,1,0:T(8,128)S(1)}, bf16[1808,128]{1,0:T(8,128)(2,1)S(1)}, f32[4,128]{1,0:T(4,128)S(1)}) custom-call(s32[1,8]{1,0:T(1,128)S(1)} %copy-done.4, bf16[528,128]{1,0:T(8,128)(2,1)S(1)} %collective-permute-done.recv, f32[6,128,128]{2,1,0:T(8,128)S(1)} %get-tuple-element.23.mh_in, ...), custom_call_target="tpu_custom_call" | custom-call | flops 1000000000 | tf_op jit(solution)/shard_map/pallas_call | solution.py:271
  11.7 15.7 %all-gather.1 = bf16[3616,128]{1,0:T(8,128)(2,1)S(1)} all-gather(bf16[1808,128]{1,0:T(8,128)(2,1)S(1)} %get-tuple-element.28), channel_id=3, replica_groups=mesh['rows'=384,'grp'=2] {'grp'}, dimensions={0}, use_global_device_ids=true | all-gather | bytes 1388544 | tf_op jit(solution)/shard_map/all_gather | solution.py:276
  27.4 0.1 shard_map.109
  27.6 1.9 %collective-permute-start.1 = (f32[2,128]{1,0:T(2,128)S(1)}, f32[2,128]{1,0:T(2,128)S(1)}, u32[]{:S(2)}, u32[]{:S(2)}) collective-permute-start(f32[2,128]{1,0:T(2,128)S(1)} %get-tuple-element.31.step), channel_id=1, source_target_pairs={{1,2},{2,1},{3,4},{4,3},{5,6},{6,5},{7,8},{8,7},{9,10},{10,9},{11,... | collective-permute-start | bytes 3080 | tf_op jit(solution)/shard_map/ppermute | solution.py:278
  29.5 0.8 %shard_map.110 = (f32[6,128,128]{2,1,0:T(8,128)S(1)}, f32[1,128]{1,0:T(1,128)S(1)}, f32[1,128,768]{2,1,0:T(8,128)}) custom-call(f32[6,128,128]{2,1,0:T(8,128)S(1)} %get-tuple-element.27.mg, bf16[2,1808,128]{2,1,0:T(8,128)(2,1)S(1)} %bitcast.7, f32[2,128]{1,0:T(2,128)S(1)} %get-tuple-element.31.step, f32[1,128]{1,0:T(1,128)S(1)} %get-tuple-element.32.base_in), custom_call_target="tpu_custom_call" | custom-call | flops 1000000000 | tf_op jit(solution)/shard_map/pallas_call | solution.py:279
  30.3 2.1 %collective-permute-done.1.refs_0_ = f32[2,128]{1,0:T(2,128)S(1)} collective-permute-done((f32[2,128]{1,0:T(2,128)S(1)}, f32[2,128]{1,0:T(2,128)S(1)}, u32[]{:S(2)}, u32[]{:S(2)}) %collective-permute-start.1) | collective-permute-done | bytes 1056 | tf_op jit(solution)/shard_map/ppermute | solution.py:278
  32.4 6.1 %all-gather.2 = f32[2,2,128]{2,1,0:T(2,128)S(1)} all-gather(f32[1,2,128]{2,1,0:T(2,128)S(1)} %bitcast.9), channel_id=1, replica_groups=mesh['rows'=384,'grp'=2] {'grp'}, dimensions={0}, use_global_device_ids=true | all-gather | bytes 3072 | tf_op jit(solution)/shard_map/all_gather | solution.py:286
  38.5 0.6 %shard_map.112 = f32[1,128]{1,0:T(1,128)} custom-call(f32[6,128,128]{2,1,0:T(8,128)S(1)} %get-tuple-element.34.mats, f32[4,128]{1,0:T(4,128)S(1)} %bitcast.8, f32[1,128]{1,0:T(1,128)S(1)} %get-tuple-element.35.refs_1_.base), custom_call_target="tpu_custom_call" | custom-call | flops 1000000000 | tf_op jit(solution)/shard_map/pallas_call | solution.py:287
  (3 shorter events, 0.0 us)
Async XLA Ops:
  0.6 0.7 %copy-start.7 = (f32[1,128]{1,0:T(1,128)S(1)}, f32[1,128]{1,0:T(1,128)}, u32[]{:S(2)}) copy-start(f32[1,128]{1,0:T(1,128)} %x.1) | copy-start | bytes 1540
  0.6 1.0 %copy-start.5 = (bf16[8,128,128]{2,1,0:T(8,128)(2,1)S(1)}, bf16[8,128,128]{2,1,0:T(8,128)(2,1)}, u32[]{:S(2)}) copy-start(bf16[8,128,128]{2,1,0:T(8,128)(2,1)} %p.1) | copy-start | bytes 786436
  0.7 0.9 %copy-start.6 = (s32[1,8]{1,0:T(1,128)S(1)}, s32[1,8]{1,0:T(1,128)}, u32[]{:S(2)}) copy-start(s32[1,8]{1,0:T(1,128)} %send.1) | copy-start | bytes 100
  1.6 6.9 %copy-start = (bf16[8,15,128,128]{3,2,1,0:T(8,128)(2,1)S(1)}, bf16[8,15,128,128]{3,2,1,0:T(8,128)(2,1)}, u32[]{:S(2)}) copy-start(bf16[8,15,128,128]{3,2,1,0:T(8,128)(2,1)} %a.1) | copy-start | bytes 11796484
  1.6 6.9 %copy-start.1 = (s32[8,15]{1,0:T(8,128)S(1)}, s32[8,15]{1,0:T(8,128)}, u32[]{:S(2)}) copy-start(s32[8,15]{1,0:T(8,128)} %cols.1) | copy-start | bytes 1444
  1.6 6.9 %copy-start.2 = (s32[1,8]{1,0:T(1,128)S(1)}, s32[1,8]{1,0:T(1,128)}, u32[]{:S(2)}) copy-start(s32[1,8]{1,0:T(1,128)} %count.1) | copy-start | bytes 100
  1.6 6.9 %copy-start.3 = (s32[8]{0:T(128)S(1)}, s32[8]{0:T(128)}, u32[]{:S(2)}) copy-start(s32[8]{0:T(128)} %cmap.1) | copy-start | bytes 100
  1.6 6.9 %copy-start.4 = (s32[1,8]{1,0:T(1,128)S(1)}, s32[1,8]{1,0:T(1,128)}, u32[]{:S(2)}) copy-start(s32[1,8]{1,0:T(1,128)} %ghost.3) | copy-start | bytes 100
  4.2 7.0 %copy-start.8 = (f32[1,128]{1,0:T(1,128)S(1)}, f32[1,128]{1,0:T(1,128)}, u32[]{:S(2)}) copy-start(f32[1,128]{1,0:T(1,128)} %rhs.1) | copy-start | bytes 1540
  4.2 6.9 %collective-permute-start = (bf16[528,128]{1,0:T(8,128)(2,1)S(1)}, bf16[528,128]{1,0:T(8,128)(2,1)S(1)}, u32[]{:S(2)}, u32[]{:S(2)}) collective-permute-start(bf16[528,128]{1,0:T(8,128)(2,1)S(1)} %get-tuple-element.21), channel_id=1, source_target_pairs={{1,2},{2,1},{3,4},{4,3},{5,6},{6,5},{7,8},{8,7},{9,10},{10,9},{11,... | collective-permute-start | bytes 405512 | tf_op jit(solution)/shard_map/ppermute | solution.py:255
  27.6 4.9 %collective-permute-start.1 = (f32[2,128]{1,0:T(2,128)S(1)}, f32[2,128]{1,0:T(2,128)S(1)}, u32[]{:S(2)}, u32[]{:S(2)}) collective-permute-start(f32[2,128]{1,0:T(2,128)S(1)} %get-tuple-element.31.step), channel_id=1, source_target_pairs={{1,2},{2,1},{3,4},{4,3},{5,6},{6,5},{7,8},{8,7},{9,10},{10,9},{11,... | collective-permute-start | bytes 3080 | tf_op jit(solution)/shard_map/ppermute | solution.py:278

commit v3 on v2

--- a/solution.py
+++ b/solution.py
@@ -14,7 +14,9 @@
 NLIVE = 40
 VECS = 16
 COARSE_US = 0
-FIRST_US = 5
+LINE = 12
+FIRST_US = 1
+SECOND_US = 1
 AFTER_US = 5
 
 THETA = 13.0
@@ -59,27 +61,22 @@
     lists = send[...]
     low = [lists[0, k] for k in range(G)]
     high = [lists[0, G + k] for k in range(G)]
-    out_a[G * B :, :] = padded(split3(x[...] + zero[0:1, :]))
+    out_b[G * B :, :] = padded(split3(x[...] + zero[0:1, :]))
     out_p[...] = p[...]
     for k in range(G):
         out_a[k * B : (k + 1) * B, :] = p[jnp.where(first, high[k], low[k])]
         out_b[k * B : (k + 1) * B, :] = p[jnp.where(first, low[k], high[k])]
 
 
-def pair_kernel(got_a, tiles, out_b, x):
-    rows = [got_a[c, G * B :, :].astype(F32) for c in range(CC)]
-    terms = [jnp.concatenate([r[k : k + 1] for r in rows], axis=0) for k in range(3)]
-    out_b[: G * B, :] = tiles[...]
-    out_b[G * B :, :] = padded(terms)
-    x[...] = terms[0] + terms[1] + terms[2]
-
-
-def coarse_kernel(cols, count, ghost, cmap, a, p, got_a, mh, mg, tb, t, pt, cols_s, count_s, ghost_s, cmap_s, sems):
+def early():
+    return lax.rem(lax.axis_index("rows"), LINE) == 0
+
+
+def own_part(cols, count, cmap, a, p, mh, mg, tab, t, pt, cols_s, count_s, cmap_s, sems):
     g = lax.axis_index("grp")
-    h = 1 - g
     copies = [
         pltpu.make_async_copy(src, dst, sems.at[n])
-        for n, (src, dst) in enumerate([(cols, cols_s), (count, count_s), (ghost, ghost_s), (cmap, cmap_s)])
+        for n, (src, dst) in enumerate([(cols, cols_s), (count, count_s), (cmap, cmap_s)])
     ]
     for copy in copies:
         copy.start()
@@ -106,18 +103,46 @@
         lo = (tc - hi.astype(F32)).astype(BF16)
         return jnp.concatenate([hi, lo], axis=1)
 
-    def add(j, lhs, tile):
-        out = jnp.dot(lhs, jnp.concatenate([tile, tile], axis=0), preferred_element_type=F32)
-        mh[j] += out[:B]
-        mg[j] += out[B:]
-
     for c in range(RB):
-        add(CC + cmap_s[c], halves(c), p[c])
-    for k in range(G):
-        q = G * h + k
-        add(ghost_s[0, q], halves(RB + q), got_a[h, k * B : (k + 1) * B, :])
-    for k in range(G):
-        tb[k] = halves(RB + G * g + k)
+        add(mh, mg, CC + cmap_s[c], halves(c), p[c])
+    for q in range(2 * G):
+        tab[q] = halves(RB + q)
+
+
+def add(mh, mg, j, lhs, tile):
+    out = jnp.dot(lhs, jnp.concatenate([tile, tile], axis=0), preferred_element_type=F32)
+    mh[j] += out[:B]
+    mg[j] += out[B:]
+
+
+def early_kernel(cols, count, cmap, a, p, pending, mh, mg, tab, passed, *scratch):
+    @pl.when(early())
+    def _():
+        own_part(cols, count, cmap, a, p, mh, mg, tab, *scratch)
+
+
+def coarse_kernel(cols, count, cmap, a, p, ghost, got_a, mh_in, mg_in, tab_in, mh, mg, tb, tab, *scratch):
+    g = lax.axis_index("grp")
+    h = 1 - g
+    lists = ghost[...]
+    js = [jnp.where(g == 0, lists[0, G + k], lists[0, k]) for k in range(G)]
+
+    def ghosts(terms):
+        for k in range(G):
+            add(mh, mg, js[k], terms[G * h + k], got_a[h, k * B : (k + 1) * B, :])
+        for k in range(G):
+            tb[k] = terms[G * g + k]
+
+    @pl.when(early())
+    def _():
+        mh[...] = mh_in[...]
+        mg[...] = mg_in[...]
+        ghosts(tab_in)
+
+    @pl.when(jnp.logical_not(early()))
+    def _():
+        own_part(cols, count, cmap, a, p, mh, mg, tab, *scratch)
+        ghosts(tab)
 
 
 def known(g):
@@ -216,14 +241,14 @@
     pass
 
 
-def after(value, *others):
+def after(value, *others, us=AFTER_US):
     (out,) = call(
         after_kernel,
         [shaped(*value.shape, dtype=value.dtype)],
         [ANY] * (1 + len(others)),
         out_specs=[ANY],
         input_output_aliases={0: 0},
-        us=AFTER_US,
+        us=us,
     )(value, *others)
     return out
 
@@ -245,29 +270,40 @@
     part = shaped(NJ, B, B)
     packed = shaped(G * B + VECS, B, dtype=BF16)
     (zero,) = call(first_kernel, [shaped(8, B)], [], us=FIRST_US)()
+    x = after(lax.all_gather(x_start, "grp", axis=0, tiled=True), us=SECOND_US)
     send_a, send_b, p = call(
         pack_kernel,
-        [packed, shaped(G * B, B, dtype=BF16), shaped(RB, B, B, dtype=BF16)],
+        [shaped(G * B, B, dtype=BF16), packed, shaped(RB, B, B, dtype=BF16)],
         [VMEM] * 4,
-    )(zero, send_lists, p_tiles, x_start)
+    )(zero, send_lists, p_tiles, x)
+    terms = shaped(2 * G, CC * B, 2 * B, dtype=BF16)
+    scratch = [
+        pltpu.VMEM((RB + 2 * G, CC, B, B), F32),
+        pltpu.VMEM((RB, B, B), BF16),
+        ints(8, 15),
+        ints(1, 8),
+        ints(8),
+        DMA((3,)),
+    ]
+    matrix = (a_cols, a_count, cmap, a_tiles, p)
+    mh, mg, tab, send_b = call(
+        early_kernel,
+        [part, part, terms, packed],
+        [HBM] * 3 + [VMEM] * 2 + [ANY],
+        scratch,
+        out_specs=[VMEM] * 3 + [ANY],
+        input_output_aliases={5: 3},
+        us=COARSE_US,
+    )(*matrix, send_b)
+    recv_b = lax.ppermute(send_b, AXES, near)
     got_a = lax.all_gather(send_a, "grp", axis=0)
-    send_b, x = call(pair_kernel, [packed, shaped(CC, B)], [VMEM] * 2)(got_a, send_b)
-    recv_b = lax.ppermute(send_b, AXES, near)
     mh, mg, tb = call(
         coarse_kernel,
         [part, part, shaped(G, CC * B, 2 * B, dtype=BF16)],
-        [HBM] * 4 + [VMEM] * 3,
-        [
-            pltpu.VMEM((RB + 2 * G, CC, B, B), F32),
-            pltpu.VMEM((RB, B, B), BF16),
-            ints(8, 15),
-            ints(1, 8),
-            ints(1, 8),
-            ints(8),
-            DMA((4,)),
-        ],
+        [HBM] * 3 + [VMEM] * 7,
+        [pltpu.VMEM((2 * G, CC * B, 2 * B), BF16)] + scratch,
         us=COARSE_US,
-    )(a_cols, a_count, ghost_cols, cmap, a_tiles, p, got_a)
+    )(*matrix, ghost_cols, got_a, mh, mg, tab)
     mh, mg, ext, vec = call(
         message_kernel,
         [part, part, shaped(14 * B + VECS, B, dtype=BF16), shaped(4, B)],

time: 39.3 us -> 38.5 us (0.980)
  blocking collectives: 24.2 us -> 26.6 us
  starting transfers between devices: 6.17 us -> 4.37 us
  local copies, waits for them, and re-layouts: 0.96 us -> 0.04 us
  waiting for transfers between devices: 2.85 us -> 2.14 us
    all_gather x1, blocking collectives: 15.7 us -> 2.77 us  [on_device(): exts = lax.all_gather(ext, 'grp', axis=0)]
    all_gather x1, blocking collectives: 2.45 us -> 15.3 us  [on_device(): got_a = lax.all_gather(send_a, 'grp', axis=0)]
    all_gather x0 -> x1, blocking collectives: none -> 2.41 us  [on_device(): x = after(lax.all_gather(x_start, 'grp', axis=0, tiled=True), us=SECOND_US)]
    ppermute x1, starting transfers between devices: 4.25 us -> 2.45 us  [on_device(): recv_b = lax.ppermute(send_b, AXES, near)]
    pallas_call x2, Pallas kernels: 0.14 us -> 1.92 us  [the longest x1 1.8 us: on_device(): call(early_kernel, [part, part, terms, packed], [HBM] * 3 + [VMEM] * 2 +...]
    pallas_call x1, Pallas kernels: 1.91 us -> 0.34 us  [on_device(): call(coarse_kernel, [part, part, shaped(G, CC * B, 2 * B, dtype=BF16)], [...]
    unnamed x18 -> x16, local copies, waits for them, and re-layouts: 0.96 us -> 0.04 us
    ppermute x1, waiting for transfers between devices: 0.71 us -> 0.01 us  [on_device(): recv_b = lax.ppermute(send_b, AXES, near)]
  transfers between devices with their start and end apart: 2 -> 2, of which waited for: 2 -> 1; matrix products, arithmetic and copies ran while one was open for 0% -> 0% of each run, Pallas kernels for 7% -> 3%
where the time goes in v3:
time: 38.5 us; the launch traced here: 38.3 us
  blocking collectives  26.6 us (69%)
  Pallas kernels  4.38 us (11%)
  starting transfers between devices  4.37 us (11%)
  waiting for transfers between devices  2.14 us (6%)
  between operations  0.8 us (2%)
    all_gather x1, blocking collectives, on_device(): got_a = lax.all_gather(send_a, 'grp', axis=0)  15.3 us
    all_gather x1, blocking collectives, on_device(): around = lax.all_gather(after(beyond, base), 'grp', axis=0, tiled=True)  6.08 us
    all_gather x1, blocking collectives, on_device(): exts = lax.all_gather(ext, 'grp', axis=0)  2.77 us
    ppermute x1, starting transfers between devices, on_device(): recv_b = lax.ppermute(send_b, AXES, near)  2.45 us
    all_gather x1, blocking collectives, on_device(): x = after(lax.all_gather(x_start, 'grp', axis=0, tiled=True), us=SECOND_US)  2.41 us
    ppermute x1, waiting for transfers between devices, on_device(): beyond = lax.ppermute(step, AXES, near)  2.14 us
    ppermute x1, starting transfers between devices, on_device(): beyond = lax.ppermute(step, AXES, near)  1.92 us
    pallas_call x1, Pallas kernels, on_device(): call(early_kernel, [part, part, terms, packed], [HBM] * 3 + [VMEM] * 2 +...  1.8 us
  transfers between devices with their start and end apart: 2, of which 1 were waited for; matrix products, arithmetic and copies ran while one was open for 0% of the time, Pallas kernels for 3%

profile of v3, /device:TPU:7, one launch (start us, length us, event | category | flops | bytes accessed | tf_op | source)
XLA Modules:
  0.0 38.3 jit_solution(14804713613109340976)
XLA Ops:
  0.6 0.0 copy-start.5
  0.6 0.0 copy-start.6
  0.7 0.0 copy-start
  0.7 0.0 copy-start.1
  0.7 0.0 copy-start.2
  0.7 0.0 copy-start.3
  0.7 2.4 %all-gather.2 = f32[2,1,128]{2,1,0:T(1,128)S(1)} all-gather(f32[1,1,128]{2,1,0:T(1,128)} %bitcast.12), channel_id=1, replica_groups=mesh['rows'=384,'grp'=2] {'grp'}, dimensions={0}, use_global_device_ids=true | all-gather | bytes 1536 | tf_op jit(solution)/shard_map/all_gather | solution.py:273
  3.1 0.0 copy-done.5
  3.1 0.0 copy-done.6
  3.1 0.0 copy-start.4
  3.1 0.1 shard_map.106
  3.3 0.0 copy-done
  3.3 0.0 copy-done.1
  3.3 0.0 copy-done.2
  3.3 0.0 copy-done.3
  3.3 1.8 %shard_map.107 = (f32[6,128,128]{2,1,0:T(8,128)S(1)}, f32[6,128,128]{2,1,0:T(8,128)S(1)}, bf16[8,256,256]{2,1,0:T(8,128)(2,1)S(1)}, bf16[528,128]{1,0:T(8,128)(2,1)S(1)}) custom-call(s32[8,15]{1,0:T(8,128)S(1)} %copy-done.1, s32[1,8]{1,0:T(1,128)S(1)} %copy-done.2, s32[8]{0:T(128)S(1)} %copy-done.3, ...), custom_call_target="tpu_custom_call", output_to_operand_aliasing={{3}: (5, {})} | custom-call | tf_op jit(solution)/shard_map/pallas_call | solution.py:289
  5.1 0.0 copy-start.7
  5.1 2.5 %collective-permute-start = (bf16[528,128]{1,0:T(8,128)(2,1)S(1)}, bf16[528,128]{1,0:T(8,128)(2,1)S(1)}, u32[]{:S(2)}, u32[]{:S(2)}) collective-permute-start(bf16[528,128]{1,0:T(8,128)(2,1)S(1)} %get-tuple-element.23), channel_id=1, source_target_pairs={{1,2},{2,1},{3,4},{4,3},{5,6},{6,5},{7,8},{8,7},{9,10},{10,9},{11,... | collective-permute-start | bytes 405512 | tf_op jit(solution)/shard_map/ppermute | solution.py:298
  7.6 15.3 %all-gather = bf16[1024,128]{1,0:T(8,128)(2,1)S(1)} all-gather(bf16[512,128]{1,0:T(8,128)(2,1)S(1)} %get-tuple-element.24), channel_id=2, replica_groups=mesh['rows'=384,'grp'=2] {'grp'}, dimensions={0}, use_global_device_ids=true | all-gather | bytes 393216 | tf_op jit(solution)/shard_map/all_gather | solution.py:299
  22.9 0.0 copy-done.4
  22.9 0.3 shard_map.108
  23.2 0.0 collective-permute-done.recv
  23.3 0.0 copy-done.7
  23.3 0.5 %shard_map.109 = (f32[6,128,128]{2,1,0:T(8,128)S(1)}, f32[6,128,128]{2,1,0:T(8,128)S(1)}, bf16[1808,128]{1,0:T(8,128)(2,1)S(1)}, f32[4,128]{1,0:T(4,128)S(1)}) custom-call(s32[1,8]{1,0:T(1,128)S(1)} %copy-done.4, bf16[528,128]{1,0:T(8,128)(2,1)S(1)} %collective-permute-done.recv, f32[6,128,128]{2,1,0:T(8,128)S(1)} %get-tuple-element.28.mh_in, ...), custom_call_target="tpu_custom_call" | custom-call | flops 1000000000 | tf_op jit(solution)/shard_map/pallas_call | solution.py:307
  23.8 2.8 %all-gather.1 = bf16[3616,128]{1,0:T(8,128)(2,1)S(1)} all-gather(bf16[1808,128]{1,0:T(8,128)(2,1)S(1)} %get-tuple-element.32), channel_id=3, replica_groups=mesh['rows'=384,'grp'=2] {'grp'}, dimensions={0}, use_global_device_ids=true | all-gather | bytes 1388544 | tf_op jit(solution)/shard_map/all_gather | solution.py:312
  26.6 0.1 shard_map.110
  26.7 1.9 %collective-permute-start.1 = (f32[2,128]{1,0:T(2,128)S(1)}, f32[2,128]{1,0:T(2,128)S(1)}, u32[]{:S(2)}, u32[]{:S(2)}) collective-permute-start(f32[2,128]{1,0:T(2,128)S(1)} %get-tuple-element.35.step), channel_id=1, source_target_pairs={{1,2},{2,1},{3,4},{4,3},{5,6},{6,5},{7,8},{8,7},{9,10},{10,9},{11,... | collective-permute-start | bytes 3080 | tf_op jit(solution)/shard_map/ppermute | solution.py:314
  28.6 0.8 %shard_map.111 = (f32[6,128,128]{2,1,0:T(8,128)S(1)}, f32[1,128]{1,0:T(1,128)S(1)}, f32[1,128,768]{2,1,0:T(8,128)}) custom-call(f32[6,128,128]{2,1,0:T(8,128)S(1)} %get-tuple-element.31.mg, bf16[2,1808,128]{2,1,0:T(8,128)(2,1)S(1)} %bitcast.8, f32[2,128]{1,0:T(2,128)S(1)} %get-tuple-element.35.step, f32[1,128]{1,0:T(1,128)S(1)} %get-tuple-element.36.base_in), custom_call_target="tpu_custom_call" | custom-call | flops 1000000000 | tf_op jit(solution)/shard_map/pallas_call | solution.py:315
  29.5 2.1 %collective-permute-done.1.refs_0_ = f32[2,128]{1,0:T(2,128)S(1)} collective-permute-done((f32[2,128]{1,0:T(2,128)S(1)}, f32[2,128]{1,0:T(2,128)S(1)}, u32[]{:S(2)}, u32[]{:S(2)}) %collective-permute-start.1) | collective-permute-done | bytes 1056 | tf_op jit(solution)/shard_map/ppermute | solution.py:314
  31.6 6.1 %all-gather.3 = f32[2,2,128]{2,1,0:T(2,128)S(1)} all-gather(f32[1,2,128]{2,1,0:T(2,128)S(1)} %bitcast.10), channel_id=1, replica_groups=mesh['rows'=384,'grp'=2] {'grp'}, dimensions={0}, use_global_device_ids=true | all-gather | bytes 3072 | tf_op jit(solution)/shard_map/all_gather | solution.py:322
  37.7 0.6 %shard_map.113 = f32[1,128]{1,0:T(1,128)} custom-call(f32[6,128,128]{2,1,0:T(8,128)S(1)} %get-tuple-element.38.mats, f32[4,128]{1,0:T(4,128)S(1)} %bitcast.9, f32[1,128]{1,0:T(1,128)S(1)} %get-tuple-element.39.refs_1_.base), custom_call_target="tpu_custom_call" | custom-call | flops 1000000000 | tf_op jit(solution)/shard_map/pallas_call | solution.py:323
  (3 shorter events, 0.0 us)
Async XLA Ops:
  0.6 2.5 %copy-start.5 = (bf16[8,128,128]{2,1,0:T(8,128)(2,1)S(1)}, bf16[8,128,128]{2,1,0:T(8,128)(2,1)}, u32[]{:S(2)}) copy-start(bf16[8,128,128]{2,1,0:T(8,128)(2,1)} %p.1) | copy-start | bytes 786436
  0.6 2.5 %copy-start.6 = (s32[1,8]{1,0:T(1,128)S(1)}, s32[1,8]{1,0:T(1,128)}, u32[]{:S(2)}) copy-start(s32[1,8]{1,0:T(1,128)} %send.1) | copy-start | bytes 100
  0.7 2.6 %copy-start = (bf16[8,15,128,128]{3,2,1,0:T(8,128)(2,1)S(1)}, bf16[8,15,128,128]{3,2,1,0:T(8,128)(2,1)}, u32[]{:S(2)}) copy-start(bf16[8,15,128,128]{3,2,1,0:T(8,128)(2,1)} %a.3) | copy-start | bytes 11796484
  0.7 2.6 %copy-start.1 = (s32[8,15]{1,0:T(8,128)S(1)}, s32[8,15]{1,0:T(8,128)}, u32[]{:S(2)}) copy-start(s32[8,15]{1,0:T(8,128)} %cols.3) | copy-start | bytes 1444
  0.7 2.6 %copy-start.2 = (s32[1,8]{1,0:T(1,128)S(1)}, s32[1,8]{1,0:T(1,128)}, u32[]{:S(2)}) copy-start(s32[1,8]{1,0:T(1,128)} %count.3) | copy-start | bytes 100
  0.7 2.6 %copy-start.3 = (s32[8]{0:T(128)S(1)}, s32[8]{0:T(128)}, u32[]{:S(2)}) copy-start(s32[8]{0:T(128)} %cmap.3) | copy-start | bytes 100
  3.1 19.8 %copy-start.4 = (s32[1,8]{1,0:T(1,128)S(1)}, s32[1,8]{1,0:T(1,128)}, u32[]{:S(2)}) copy-start(s32[1,8]{1,0:T(1,128)} %ghost.3) | copy-start | bytes 100
  5.1 18.1 %copy-start.7 = (f32[1,128]{1,0:T(1,128)S(1)}, f32[1,128]{1,0:T(1,128)}, u32[]{:S(2)}) copy-start(f32[1,128]{1,0:T(1,128)} %rhs.1) | copy-start | bytes 1540
  5.1 18.1 %collective-permute-start = (bf16[528,128]{1,0:T(8,128)(2,1)S(1)}, bf16[528,128]{1,0:T(8,128)(2,1)S(1)}, u32[]{:S(2)}, u32[]{:S(2)}) collective-permute-start(bf16[528,128]{1,0:T(8,128)(2,1)S(1)} %get-tuple-element.23), channel_id=1, source_target_pairs={{1,2},{2,1},{3,4},{4,3},{5,6},{6,5},{7,8},{8,7},{9,10},{10,9},{11,... | collective-permute-start | bytes 405512 | tf_op jit(solution)/shard_map/ppermute | solution.py:298
  26.7 4.9 %collective-permute-start.1 = (f32[2,128]{1,0:T(2,128)S(1)}, f32[2,128]{1,0:T(2,128)S(1)}, u32[]{:S(2)}, u32[]{:S(2)}) collective-permute-start(f32[2,128]{1,0:T(2,128)S(1)} %get-tuple-element.35.step), channel_id=1, source_target_pairs={{1,2},{2,1},{3,4},{4,3},{5,6},{6,5},{7,8},{8,7},{9,10},{10,9},{11,... | collective-permute-start | bytes 3080 | tf_op jit(solution)/shard_map/ppermute | solution.py:314

commit v4 on v3

--- a/solution.py
+++ b/solution.py
@@ -54,18 +54,6 @@
 
 def first_kernel(out):
     out[...] = jnp.zeros_like(out)
-
-
-def pack_kernel(zero, send, p, x, out_a, out_b, out_p):
-    first = lax.axis_index("grp") == 0
-    lists = send[...]
-    low = [lists[0, k] for k in range(G)]
-    high = [lists[0, G + k] for k in range(G)]
-    out_b[G * B :, :] = padded(split3(x[...] + zero[0:1, :]))
-    out_p[...] = p[...]
-    for k in range(G):
-        out_a[k * B : (k + 1) * B, :] = p[jnp.where(first, high[k], low[k])]
-        out_b[k * B : (k + 1) * B, :] = p[jnp.where(first, low[k], high[k])]
 
 
 def early():
@@ -115,7 +103,21 @@
     mg[j] += out[B:]
 
 
-def early_kernel(cols, count, cmap, a, p, pending, mh, mg, tab, passed, *scratch):
+def pack(zero, send, p, x, out_a, out_b, out_p):
+    first = lax.axis_index("grp") == 0
+    lists = send[...]
+    low = [lists[0, k] for k in range(G)]
+    high = [lists[0, G + k] for k in range(G)]
+    out_b[G * B :, :] = padded(split3(x[...] + zero[0:1, :]))
+    out_p[...] = p[...]
+    for k in range(G):
+        out_a[k * B : (k + 1) * B, :] = p[jnp.where(first, high[k], low[k])]
+        out_b[k * B : (k + 1) * B, :] = p[jnp.where(first, low[k], high[k])]
+
+
+def early_kernel(zero, send, x, cols, count, cmap, a, p, out_a, out_b, out_p, mh, mg, tab, *scratch):
+    pack(zero, send, p, x, out_a, out_b, out_p)
+
     @pl.when(early())
     def _():
         own_part(cols, count, cmap, a, p, mh, mg, tab, *scratch)
@@ -171,32 +173,27 @@
     w_h = matvec([mh[j] for j in js], xs)
     w_g = matvec([mg[j] for j in js], xs)
     for j in range(NJ):
-        hi = mh[j].astype(BF16)
-        ext[j * B : (j + 1) * B, :] = hi
-        ext[(NJ + j) * B : (NJ + j + 1) * B, :] = (mh[j] - hi.astype(F32)).astype(BF16)
+        ext[j * B : (j + 1) * B, :] = mh[j].astype(BF16)
     for q, j in enumerate(known(1 - g)):
-        ext[(2 * NJ + q) * B : (2 * NJ + q + 1) * B, :] = mg[j].astype(BF16)
+        ext[(NJ + q) * B : (NJ + q + 1) * B, :] = mg[j].astype(BF16)
     rows = jnp.concatenate([w_h, rhs[...] - w_g, near], axis=0)
-    ext[14 * B :, :] = padded(split3(rows))
+    ext[8 * B :, :] = padded(split3(rows))
     vec[...] = rows
 
 
 def wide(exts, c, j):
-    return (
-        exts[c, pl.ds(pl.multiple_of(j * B, B), B), :].astype(F32)
-        + exts[c, pl.ds(pl.multiple_of((NJ + j) * B, B), B), :].astype(F32)
-    )
+    return exts[c, pl.ds(pl.multiple_of(j * B, B), B), :].astype(F32)
 
 
 def step_kernel(exts, mh, mg, vec, x, step, base):
     g = lax.axis_index("grp")
     h = 1 - g
     first = g == 0
-    rows = exts[h, 14 * B :, :].astype(F32)
+    rows = exts[h, 8 * B :, :].astype(F32)
     far = rows[0:4] + rows[4:8] + rows[8:12]
     xs = [far[2:3], far[3:4], vec[2:3, :], vec[3:4, :]]
     in_g = [mg[j] for j in known(h)] + [wide(exts, h, j) for j in known(g)]
-    in_h = [mh[j] for j in known(h)] + [exts[h, (12 + q) * B : (13 + q) * B, :].astype(F32) for q in range(CC)]
+    in_h = [mh[j] for j in known(h)] + [exts[h, (NJ + q) * B : (NJ + q + 1) * B, :].astype(F32) for q in range(CC)]
     resid = vec[1:2, :] - far[0:1] - matvec(in_g, xs)
     resid_h = far[1:2] - vec[0:1, :] - matvec(in_h, xs)
     d_g = resid / THETA
@@ -271,11 +268,6 @@
     packed = shaped(G * B + VECS, B, dtype=BF16)
     (zero,) = call(first_kernel, [shaped(8, B)], [], us=FIRST_US)()
     x = after(lax.all_gather(x_start, "grp", axis=0, tiled=True), us=SECOND_US)
-    send_a, send_b, p = call(
-        pack_kernel,
-        [shaped(G * B, B, dtype=BF16), packed, shaped(RB, B, B, dtype=BF16)],
-        [VMEM] * 4,
-    )(zero, send_lists, p_tiles, x)
     terms = shaped(2 * G, CC * B, 2 * B, dtype=BF16)
     scratch = [
         pltpu.VMEM((RB + 2 * G, CC, B, B), F32),
@@ -285,16 +277,14 @@
         ints(8),
         DMA((3,)),
     ]
-    matrix = (a_cols, a_count, cmap, a_tiles, p)
-    mh, mg, tab, send_b = call(
+    matrix = (a_cols, a_count, cmap, a_tiles)
+    send_a, send_b, p, mh, mg, tab = call(
         early_kernel,
-        [part, part, terms, packed],
-        [HBM] * 3 + [VMEM] * 2 + [ANY],
+        [shaped(G * B, B, dtype=BF16), packed, shaped(RB, B, B, dtype=BF16), part, part, terms],
+        [VMEM] * 3 + [HBM] * 3 + [VMEM] * 2,
         scratch,
-        out_specs=[VMEM] * 3 + [ANY],
-        input_output_aliases={5: 3},
         us=COARSE_US,
-    )(*matrix, send_b)
+    )(zero, send_lists, x, *matrix, p_tiles)
     recv_b = lax.ppermute(send_b, AXES, near)
     got_a = lax.all_gather(send_a, "grp", axis=0)
     mh, mg, tb = call(
@@ -303,10 +293,10 @@
         [HBM] * 3 + [VMEM] * 7,
         [pltpu.VMEM((2 * G, CC * B, 2 * B), BF16)] + scratch,
         us=COARSE_US,
-    )(*matrix, ghost_cols, got_a, mh, mg, tab)
+    )(*matrix, p, ghost_cols, got_a, mh, mg, tab)
     mh, mg, ext, vec = call(
         message_kernel,
-        [part, part, shaped(14 * B + VECS, B, dtype=BF16), shaped(4, B)],
+        [part, part, shaped(8 * B + VECS, B, dtype=BF16), shaped(4, B)],
         [VMEM] * 7,
     )(ghost_cols, recv_b, mh, mg, tb, x, coarse_rhs)
     exts = lax.all_gather(ext, "grp", axis=0)

time: 38.5 us -> 38.1 us (0.990)
    pallas_call x3 -> x2, Pallas kernels: 2.46 us -> 2.37 us  [the longest x1 1.92 us: on_device(): call(early_kernel, [shaped(G * B, B, dtype=BF16), packed, shaped(RB, B, B...]
where the time goes in v4:
time: 38.1 us; the launch traced here: 37.9 us
  blocking collectives  26.3 us (69%)
  starting transfers between devices  4.39 us (12%)
  Pallas kernels  4.29 us (11%)
  waiting for transfers between devices  2.15 us (6%)
  between operations  0.8 us (2%)
    all_gather x1, blocking collectives, on_device(): got_a = lax.all_gather(send_a, 'grp', axis=0)  15.3 us
    all_gather x1, blocking collectives, on_device(): around = lax.all_gather(after(beyond, base), 'grp', axis=0, tiled=True)  6.08 us
    all_gather x1, blocking collectives, on_device(): exts = lax.all_gather(ext, 'grp', axis=0)  2.48 us
    ppermute x1, starting transfers between devices, on_device(): recv_b = lax.ppermute(send_b, AXES, near)  2.47 us
    all_gather x1, blocking collectives, on_device(): x = after(lax.all_gather(x_start, 'grp', axis=0, tiled=True), us=SECOND_US)  2.41 us
    ppermute x1, waiting for transfers between devices, on_device(): beyond = lax.ppermute(step, AXES, near)  2.14 us
    ppermute x1, starting transfers between devices, on_device(): beyond = lax.ppermute(step, AXES, near)  1.92 us
    pallas_call x1, Pallas kernels, on_device(): call(early_kernel, [shaped(G * B, B, dtype=BF16), packed, shaped(RB, B, B...  1.92 us
  transfers between devices with their start and end apart: 2, of which 1 were waited for; matrix products, arithmetic and copies ran while one was open for 0% of the time, Pallas kernels for 3%

profile of v4, /device:TPU:7, one launch (start us, length us, event | category | flops | bytes accessed | tf_op | source)
XLA Modules:
  0.0 37.9 jit_solution(11613107515783252029)
XLA Ops:
  0.6 0.0 copy-start.4
  0.6 0.0 copy-start.3
  0.7 0.0 copy-start.2
  0.7 0.0 copy-start
  0.7 0.0 copy-start.1
  0.7 0.0 copy-start.5
  0.7 2.4 %all-gather.2 = f32[2,1,128]{2,1,0:T(1,128)S(1)} all-gather(f32[1,1,128]{2,1,0:T(1,128)} %bitcast.12), channel_id=1, replica_groups=mesh['rows'=384,'grp'=2] {'grp'}, dimensions={0}, use_global_device_ids=true | all-gather | bytes 1536 | tf_op jit(solution)/shard_map/all_gather | solution.py:270
  3.1 0.0 copy-start.6
  3.1 0.0 copy-done.4
  3.1 0.0 copy-done.3
  3.1 0.0 copy-done.2
  3.1 0.0 copy-done
  3.1 0.0 copy-done.1
  3.2 0.0 copy-done.5
  3.2 1.9 %shard_map.106 = (bf16[512,128]{1,0:T(8,128)(2,1)S(1)}, bf16[528,128]{1,0:T(8,128)(2,1)S(1)}, bf16[8,128,128]{2,1,0:T(8,128)(2,1)S(1)}, f32[6,128,128]{2,1,0:T(8...) custom-call(f32[8,128]{1,0:T(8,128)S(1)} %shard_map.104.zero, s32[1,8]{1,0:T(1,128)S(1)} %copy-done.5, ...), custom_call_target="tpu_custom_call" | custom-call | tf_op jit(solution)/shard_map/pallas_call | solution.py:281
  5.1 0.0 copy-start.7
  5.1 2.5 %collective-permute-start = (bf16[528,128]{1,0:T(8,128)(2,1)S(1)}, bf16[528,128]{1,0:T(8,128)(2,1)S(1)}, u32[]{:S(2)}, u32[]{:S(2)}) collective-permute-start(bf16[528,128]{1,0:T(8,128)(2,1)S(1)} %get-tuple-element.20), channel_id=1, source_target_pairs={{1,2},{2,1},{3,4},{4,3},{5,6},{6,5},{7,8},{8,7},{9,10},{10,9},{11,... | collective-permute-start | bytes 405512 | tf_op jit(solution)/shard_map/ppermute | solution.py:288
  7.6 15.3 %all-gather = bf16[1024,128]{1,0:T(8,128)(2,1)S(1)} all-gather(bf16[512,128]{1,0:T(8,128)(2,1)S(1)} %get-tuple-element.22), channel_id=2, replica_groups=mesh['rows'=384,'grp'=2] {'grp'}, dimensions={0}, use_global_device_ids=true | all-gather | bytes 393216 | tf_op jit(solution)/shard_map/all_gather | solution.py:289
  22.8 0.0 copy-done.6
  22.9 0.3 shard_map.107
  23.2 0.0 collective-permute-done.recv
  23.2 0.0 copy-done.7
  23.2 0.5 %shard_map.108 = (f32[6,128,128]{2,1,0:T(8,128)S(1)}, f32[6,128,128]{2,1,0:T(8,128)S(1)}, bf16[1040,128]{1,0:T(8,128)(2,1)S(1)}, f32[4,128]{1,0:T(4,128)S(1)}) custom-call(s32[1,8]{1,0:T(1,128)S(1)} %copy-done.6, bf16[528,128]{1,0:T(8,128)(2,1)S(1)} %collective-permute-done.recv, f32[6,128,128]{2,1,0:T(8,128)S(1)} %get-tuple-element.26.mh_in, ...), custom_call_target="tpu_custom_call" | custom-call | flops 1000000000 | tf_op jit(solution)/shard_map/pallas_call | solution.py:297
  23.7 2.5 %all-gather.1 = bf16[2080,128]{1,0:T(8,128)(2,1)S(1)} all-gather(bf16[1040,128]{1,0:T(8,128)(2,1)S(1)} %get-tuple-element.30), channel_id=3, replica_groups=mesh['rows'=384,'grp'=2] {'grp'}, dimensions={0}, use_global_device_ids=true | all-gather | bytes 798720 | tf_op jit(solution)/shard_map/all_gather | solution.py:302
  26.2 0.1 shard_map.109
  26.3 1.9 %collective-permute-start.1 = (f32[2,128]{1,0:T(2,128)S(1)}, f32[2,128]{1,0:T(2,128)S(1)}, u32[]{:S(2)}, u32[]{:S(2)}) collective-permute-start(f32[2,128]{1,0:T(2,128)S(1)} %get-tuple-element.33.step), channel_id=1, source_target_pairs={{1,2},{2,1},{3,4},{4,3},{5,6},{6,5},{7,8},{8,7},{9,10},{10,9},{11,... | collective-permute-start | bytes 3080 | tf_op jit(solution)/shard_map/ppermute | solution.py:304
  28.2 0.8 %shard_map.110 = (f32[6,128,128]{2,1,0:T(8,128)S(1)}, f32[1,128]{1,0:T(1,128)S(1)}, f32[1,128,768]{2,1,0:T(8,128)}) custom-call(f32[6,128,128]{2,1,0:T(8,128)S(1)} %get-tuple-element.29.mg, bf16[2,1040,128]{2,1,0:T(8,128)(2,1)S(1)} %bitcast.8, f32[2,128]{1,0:T(2,128)S(1)} %get-tuple-element.33.step, f32[1,128]{1,0:T(1,128)S(1)} %get-tuple-element.34.base_in), custom_call_target="tpu_custom_call" | custom-call | flops 1000000000 | tf_op jit(solution)/shard_map/pallas_call | solution.py:305
  29.0 2.1 %collective-permute-done.1.refs_0_ = f32[2,128]{1,0:T(2,128)S(1)} collective-permute-done((f32[2,128]{1,0:T(2,128)S(1)}, f32[2,128]{1,0:T(2,128)S(1)}, u32[]{:S(2)}, u32[]{:S(2)}) %collective-permute-start.1) | collective-permute-done | bytes 1056 | tf_op jit(solution)/shard_map/ppermute | solution.py:304
  31.2 6.1 %all-gather.3 = f32[2,2,128]{2,1,0:T(2,128)S(1)} all-gather(f32[1,2,128]{2,1,0:T(2,128)S(1)} %bitcast.10), channel_id=1, replica_groups=mesh['rows'=384,'grp'=2] {'grp'}, dimensions={0}, use_global_device_ids=true | all-gather | bytes 3072 | tf_op jit(solution)/shard_map/all_gather | solution.py:312
  37.3 0.6 %shard_map.112 = f32[1,128]{1,0:T(1,128)} custom-call(f32[6,128,128]{2,1,0:T(8,128)S(1)} %get-tuple-element.36.mats, f32[4,128]{1,0:T(4,128)S(1)} %bitcast.9, f32[1,128]{1,0:T(1,128)S(1)} %get-tuple-element.37.refs_1_.base), custom_call_target="tpu_custom_call" | custom-call | flops 1000000000 | tf_op jit(solution)/shard_map/pallas_call | solution.py:313
  (3 shorter events, 0.0 us)
Async XLA Ops:
  0.6 2.5 %copy-start.4 = (s32[8]{0:T(128)S(1)}, s32[8]{0:T(128)}, u32[]{:S(2)}) copy-start(s32[8]{0:T(128)} %cmap.3) | copy-start | bytes 100
  0.6 2.5 %copy-start.3 = (s32[1,8]{1,0:T(1,128)S(1)}, s32[1,8]{1,0:T(1,128)}, u32[]{:S(2)}) copy-start(s32[1,8]{1,0:T(1,128)} %count.3) | copy-start | bytes 100
  0.7 2.5 %copy-start.2 = (s32[8,15]{1,0:T(8,128)S(1)}, s32[8,15]{1,0:T(8,128)}, u32[]{:S(2)}) copy-start(s32[8,15]{1,0:T(8,128)} %cols.3) | copy-start | bytes 1444
  0.7 2.5 %copy-start = (bf16[8,15,128,128]{3,2,1,0:T(8,128)(2,1)S(1)}, bf16[8,15,128,128]{3,2,1,0:T(8,128)(2,1)}, u32[]{:S(2)}) copy-start(bf16[8,15,128,128]{3,2,1,0:T(8,128)(2,1)} %a.3) | copy-start | bytes 11796484
  0.7 2.5 %copy-start.1 = (bf16[8,128,128]{2,1,0:T(8,128)(2,1)S(1)}, bf16[8,128,128]{2,1,0:T(8,128)(2,1)}, u32[]{:S(2)}) copy-start(bf16[8,128,128]{2,1,0:T(8,128)(2,1)} %p.1) | copy-start | bytes 786436
  0.7 2.5 %copy-start.5 = (s32[1,8]{1,0:T(1,128)S(1)}, s32[1,8]{1,0:T(1,128)}, u32[]{:S(2)}) copy-start(s32[1,8]{1,0:T(1,128)} %send.1) | copy-start | bytes 100
  3.1 19.7 %copy-start.6 = (s32[1,8]{1,0:T(1,128)S(1)}, s32[1,8]{1,0:T(1,128)}, u32[]{:S(2)}) copy-start(s32[1,8]{1,0:T(1,128)} %ghost.3) | copy-start | bytes 100
  5.1 18.1 %copy-start.7 = (f32[1,128]{1,0:T(1,128)S(1)}, f32[1,128]{1,0:T(1,128)}, u32[]{:S(2)}) copy-start(f32[1,128]{1,0:T(1,128)} %rhs.1) | copy-start | bytes 1540
  5.1 18.1 %collective-permute-start = (bf16[528,128]{1,0:T(8,128)(2,1)S(1)}, bf16[528,128]{1,0:T(8,128)(2,1)S(1)}, u32[]{:S(2)}, u32[]{:S(2)}) collective-permute-start(bf16[528,128]{1,0:T(8,128)(2,1)S(1)} %get-tuple-element.20), channel_id=1, source_target_pairs={{1,2},{2,1},{3,4},{4,3},{5,6},{6,5},{7,8},{8,7},{9,10},{10,9},{11,... | collective-permute-start | bytes 405512 | tf_op jit(solution)/shard_map/ppermute | solution.py:288
  26.3 4.9 %collective-permute-start.1 = (f32[2,128]{1,0:T(2,128)S(1)}, f32[2,128]{1,0:T(2,128)S(1)}, u32[]{:S(2)}, u32[]{:S(2)}) collective-permute-start(f32[2,128]{1,0:T(2,128)S(1)} %get-tuple-element.33.step), channel_id=1, source_target_pairs={{1,2},{2,1},{3,4},{4,3},{5,6},{6,5},{7,8},{8,7},{9,10},{10,9},{11,... | collective-permute-start | bytes 3080 | tf_op jit(solution)/shard_map/ppermute | solution.py:304

commit v5 on v4

--- a/solution.py
+++ b/solution.py
@@ -151,27 +151,28 @@
     return [4 * g, 4 * g + 1]
 
 
-def message_kernel(ghost, recv, mh_in, mg_in, tb, x, rhs, mh, mg, ext, vec):
+def message_kernel(ghost, recv, mh_in, mg_in, tb, x, rhs, mh, mg, ext, vec, table):
     g = lax.axis_index("grp")
     first = g == 0
     lists = ghost[...]
     js = [jnp.where(first, lists[0, k], lists[0, G + k]) for k in range(G)]
-    mh[...] = mh_in[...]
-    mg[...] = mg_in[...]
+    rows = recv[G * B :, :].astype(F32)
+    near = rows[0:2] + rows[2:4] + rows[4:6]
+    none = jnp.zeros_like(near)
+    table[...] = jnp.concatenate([jnp.where(first, near, none), x[...], jnp.where(first, none, near), none], axis=0)
     outs = []
     for k in range(G):
         tile = recv[k * B : (k + 1) * B, :]
         outs.append(jnp.dot(tb[k], jnp.concatenate([tile, tile], axis=0), preferred_element_type=F32))
+    xs = [x[0:1, :], x[1:2, :], near[0:1], near[1:2]] + [table[pl.ds(js[k], 1), :] for k in range(G)]
+    at = [2, 3] + known(g)
+    w_h = matvec([mh_in[j] for j in at] + [out[:B] for out in outs], xs)
+    w_g = matvec([mg_in[j] for j in at] + [out[B:] for out in outs], xs)
+    mh[...] = mh_in[...]
+    mg[...] = mg_in[...]
     for k in range(G):
-        j = js[k]
-        mh[j] += outs[k][:B]
-        mg[j] += outs[k][B:]
-    rows = recv[G * B :, :].astype(F32)
-    near = rows[0:2] + rows[2:4] + rows[4:6]
-    xs = [x[0:1, :], x[1:2, :], near[0:1], near[1:2]]
-    js = [2, 3] + known(g)
-    w_h = matvec([mh[j] for j in js], xs)
-    w_g = matvec([mg[j] for j in js], xs)
+        mh[js[k]] += outs[k][:B]
+        mg[js[k]] += outs[k][B:]
     for j in range(NJ):
         ext[j * B : (j + 1) * B, :] = mh[j].astype(BF16)
     for q, j in enumerate(known(1 - g)):
@@ -298,6 +299,7 @@
         message_kernel,
         [part, part, shaped(8 * B + VECS, B, dtype=BF16), shaped(4, B)],
         [VMEM] * 7,
+        [pltpu.VMEM((8, B), F32)],
     )(ghost_cols, recv_b, mh, mg, tb, x, coarse_rhs)
     exts = lax.all_gather(ext, "grp", axis=0)
     step, base = call(step_kernel, [shaped(CC, B), shaped(1, B)], [VMEM] * 5)(exts, mh, mg, vec, x)

time: 38.1 us -> 38 us (level)
  no operation moved by 1% of the time
where the time goes in v5:
time: 38 us; the launch traced here: 37.8 us
  blocking collectives  26.3 us (69%)
  starting transfers between devices  4.38 us (12%)
  Pallas kernels  4.24 us (11%)
  waiting for transfers between devices  2.15 us (6%)
  between operations  0.79 us (2%)
    all_gather x1, blocking collectives, on_device(): got_a = lax.all_gather(send_a, 'grp', axis=0)  15.3 us
    all_gather x1, blocking collectives, on_device(): around = lax.all_gather(after(beyond, base), 'grp', axis=0, tiled=True)  6.09 us
    all_gather x1, blocking collectives, on_device(): exts = lax.all_gather(ext, 'grp', axis=0)  2.48 us
    ppermute x1, starting transfers between devices, on_device(): recv_b = lax.ppermute(send_b, AXES, near)  2.46 us
    all_gather x1, blocking collectives, on_device(): x = after(lax.all_gather(x_start, 'grp', axis=0, tiled=True), us=SECOND_US)  2.41 us
    ppermute x1, waiting for transfers between devices, on_device(): beyond = lax.ppermute(step, AXES, near)  2.14 us
    pallas_call x1, Pallas kernels, on_device(): call(early_kernel, [shaped(G * B, B, dtype=BF16), packed, shaped(RB, B, B...  1.92 us
    ppermute x1, starting transfers between devices, on_device(): beyond = lax.ppermute(step, AXES, near)  1.92 us
  transfers between devices with their start and end apart: 2, of which 1 were waited for; matrix products, arithmetic and copies ran while one was open for 0% of the time, Pallas kernels for 3%

profile of v5, /device:TPU:7, one launch (start us, length us, event | category | flops | bytes accessed | tf_op | source)
XLA Modules:
  0.0 37.8 jit_solution(3623477252643104452)
XLA Ops:
  0.6 0.0 copy-start.4
  0.6 0.0 copy-start.3
  0.7 0.0 copy-start.2
  0.7 0.0 copy-start
  0.7 0.0 copy-start.1
  0.7 0.0 copy-start.5
  0.7 2.4 %all-gather.2 = f32[2,1,128]{2,1,0:T(1,128)S(1)} all-gather(f32[1,1,128]{2,1,0:T(1,128)} %bitcast.12), channel_id=1, replica_groups=mesh['rows'=384,'grp'=2] {'grp'}, dimensions={0}, use_global_device_ids=true | all-gather | bytes 1536 | tf_op jit(solution)/shard_map/all_gather | solution.py:271
  3.1 0.0 copy-start.6
  3.1 0.0 copy-done.4
  3.1 0.0 copy-done.3
  3.1 0.0 copy-done.2
  3.1 0.0 copy-done
  3.1 0.0 copy-done.1
  3.2 0.0 copy-done.5
  3.2 1.9 %shard_map.106 = (bf16[512,128]{1,0:T(8,128)(2,1)S(1)}, bf16[528,128]{1,0:T(8,128)(2,1)S(1)}, bf16[8,128,128]{2,1,0:T(8,128)(2,1)S(1)}, f32[6,128,128]{2,1,0:T(8...) custom-call(f32[8,128]{1,0:T(8,128)S(1)} %shard_map.104.zero, s32[1,8]{1,0:T(1,128)S(1)} %copy-done.5, ...), custom_call_target="tpu_custom_call" | custom-call | tf_op jit(solution)/shard_map/pallas_call | solution.py:282
  5.1 0.0 copy-start.7
  5.1 2.5 %collective-permute-start = (bf16[528,128]{1,0:T(8,128)(2,1)S(1)}, bf16[528,128]{1,0:T(8,128)(2,1)S(1)}, u32[]{:S(2)}, u32[]{:S(2)}) collective-permute-start(bf16[528,128]{1,0:T(8,128)(2,1)S(1)} %get-tuple-element.20), channel_id=1, source_target_pairs={{1,2},{2,1},{3,4},{4,3},{5,6},{6,5},{7,8},{8,7},{9,10},{10,9},{11,... | collective-permute-start | bytes 405512 | tf_op jit(solution)/shard_map/ppermute | solution.py:289
  7.6 15.3 %all-gather = bf16[1024,128]{1,0:T(8,128)(2,1)S(1)} all-gather(bf16[512,128]{1,0:T(8,128)(2,1)S(1)} %get-tuple-element.22), channel_id=2, replica_groups=mesh['rows'=384,'grp'=2] {'grp'}, dimensions={0}, use_global_device_ids=true | all-gather | bytes 393216 | tf_op jit(solution)/shard_map/all_gather | solution.py:290
  22.8 0.0 copy-done.6
  22.9 0.3 shard_map.107
  23.2 0.0 collective-permute-done.recv
  23.2 0.0 copy-done.7
  23.2 0.4 %shard_map.108 = (f32[6,128,128]{2,1,0:T(8,128)S(1)}, f32[6,128,128]{2,1,0:T(8,128)S(1)}, bf16[1040,128]{1,0:T(8,128)(2,1)S(1)}, f32[4,128]{1,0:T(4,128)S(1)}) custom-call(s32[1,8]{1,0:T(1,128)S(1)} %copy-done.6, bf16[528,128]{1,0:T(8,128)(2,1)S(1)} %collective-permute-done.recv, f32[6,128,128]{2,1,0:T(8,128)S(1)} %get-tuple-element.26.mh_in, ...), custom_call_target="tpu_custom_call" | custom-call | flops 1000000000 | tf_op jit(solution)/shard_map/pallas_call | solution.py:298
  23.6 2.5 %all-gather.1 = bf16[2080,128]{1,0:T(8,128)(2,1)S(1)} all-gather(bf16[1040,128]{1,0:T(8,128)(2,1)S(1)} %get-tuple-element.30), channel_id=3, replica_groups=mesh['rows'=384,'grp'=2] {'grp'}, dimensions={0}, use_global_device_ids=true | all-gather | bytes 798720 | tf_op jit(solution)/shard_map/all_gather | solution.py:304
  26.1 0.1 shard_map.109
  26.2 1.9 %collective-permute-start.1 = (f32[2,128]{1,0:T(2,128)S(1)}, f32[2,128]{1,0:T(2,128)S(1)}, u32[]{:S(2)}, u32[]{:S(2)}) collective-permute-start(f32[2,128]{1,0:T(2,128)S(1)} %get-tuple-element.33.step), channel_id=1, source_target_pairs={{1,2},{2,1},{3,4},{4,3},{5,6},{6,5},{7,8},{8,7},{9,10},{10,9},{11,... | collective-permute-start | bytes 3080 | tf_op jit(solution)/shard_map/ppermute | solution.py:306
  28.2 0.8 %shard_map.110 = (f32[6,128,128]{2,1,0:T(8,128)S(1)}, f32[1,128]{1,0:T(1,128)S(1)}, f32[1,128,768]{2,1,0:T(8,128)}) custom-call(f32[6,128,128]{2,1,0:T(8,128)S(1)} %get-tuple-element.29.mg, bf16[2,1040,128]{2,1,0:T(8,128)(2,1)S(1)} %bitcast.8, f32[2,128]{1,0:T(2,128)S(1)} %get-tuple-element.33.step, f32[1,128]{1,0:T(1,128)S(1)} %get-tuple-element.34.base_in), custom_call_target="tpu_custom_call" | custom-call | flops 1000000000 | tf_op jit(solution)/shard_map/pallas_call | solution.py:307
  29.0 2.1 %collective-permute-done.1.refs_0_ = f32[2,128]{1,0:T(2,128)S(1)} collective-permute-done((f32[2,128]{1,0:T(2,128)S(1)}, f32[2,128]{1,0:T(2,128)S(1)}, u32[]{:S(2)}, u32[]{:S(2)}) %collective-permute-start.1) | collective-permute-done | bytes 1056 | tf_op jit(solution)/shard_map/ppermute | solution.py:306
  31.1 6.1 %all-gather.3 = f32[2,2,128]{2,1,0:T(2,128)S(1)} all-gather(f32[1,2,128]{2,1,0:T(2,128)S(1)} %bitcast.10), channel_id=1, replica_groups=mesh['rows'=384,'grp'=2] {'grp'}, dimensions={0}, use_global_device_ids=true | all-gather | bytes 3072 | tf_op jit(solution)/shard_map/all_gather | solution.py:314
  37.2 0.6 %shard_map.112 = f32[1,128]{1,0:T(1,128)} custom-call(f32[6,128,128]{2,1,0:T(8,128)S(1)} %get-tuple-element.36.mats, f32[4,128]{1,0:T(4,128)S(1)} %bitcast.9, f32[1,128]{1,0:T(1,128)S(1)} %get-tuple-element.37.refs_1_.base), custom_call_target="tpu_custom_call" | custom-call | flops 1000000000 | tf_op jit(solution)/shard_map/pallas_call | solution.py:315
  (3 shorter events, 0.0 us)
Async XLA Ops:
  0.6 2.5 %copy-start.4 = (s32[8]{0:T(128)S(1)}, s32[8]{0:T(128)}, u32[]{:S(2)}) copy-start(s32[8]{0:T(128)} %cmap.3) | copy-start | bytes 100
  0.6 2.5 %copy-start.3 = (s32[1,8]{1,0:T(1,128)S(1)}, s32[1,8]{1,0:T(1,128)}, u32[]{:S(2)}) copy-start(s32[1,8]{1,0:T(1,128)} %count.3) | copy-start | bytes 100
  0.7 2.5 %copy-start.2 = (s32[8,15]{1,0:T(8,128)S(1)}, s32[8,15]{1,0:T(8,128)}, u32[]{:S(2)}) copy-start(s32[8,15]{1,0:T(8,128)} %cols.3) | copy-start | bytes 1444
  0.7 2.5 %copy-start = (bf16[8,15,128,128]{3,2,1,0:T(8,128)(2,1)S(1)}, bf16[8,15,128,128]{3,2,1,0:T(8,128)(2,1)}, u32[]{:S(2)}) copy-start(bf16[8,15,128,128]{3,2,1,0:T(8,128)(2,1)} %a.3) | copy-start | bytes 11796484
  0.7 2.5 %copy-start.1 = (bf16[8,128,128]{2,1,0:T(8,128)(2,1)S(1)}, bf16[8,128,128]{2,1,0:T(8,128)(2,1)}, u32[]{:S(2)}) copy-start(bf16[8,128,128]{2,1,0:T(8,128)(2,1)} %p.1) | copy-start | bytes 786436
  0.7 2.5 %copy-start.5 = (s32[1,8]{1,0:T(1,128)S(1)}, s32[1,8]{1,0:T(1,128)}, u32[]{:S(2)}) copy-start(s32[1,8]{1,0:T(1,128)} %send.1) | copy-start | bytes 100
  3.1 19.7 %copy-start.6 = (s32[1,8]{1,0:T(1,128)S(1)}, s32[1,8]{1,0:T(1,128)}, u32[]{:S(2)}) copy-start(s32[1,8]{1,0:T(1,128)} %ghost.3) | copy-start | bytes 100
  5.1 18.1 %copy-start.7 = (f32[1,128]{1,0:T(1,128)S(1)}, f32[1,128]{1,0:T(1,128)}, u32[]{:S(2)}) copy-start(f32[1,128]{1,0:T(1,128)} %rhs.1) | copy-start | bytes 1540
  5.1 18.1 %collective-permute-start = (bf16[528,128]{1,0:T(8,128)(2,1)S(1)}, bf16[528,128]{1,0:T(8,128)(2,1)S(1)}, u32[]{:S(2)}, u32[]{:S(2)}) collective-permute-start(bf16[528,128]{1,0:T(8,128)(2,1)S(1)} %get-tuple-element.20), channel_id=1, source_target_pairs={{1,2},{2,1},{3,4},{4,3},{5,6},{6,5},{7,8},{8,7},{9,10},{10,9},{11,... | collective-permute-start | bytes 405512 | tf_op jit(solution)/shard_map/ppermute | solution.py:289
  26.2 4.9 %collective-permute-start.1 = (f32[2,128]{1,0:T(2,128)S(1)}, f32[2,128]{1,0:T(2,128)S(1)}, u32[]{:S(2)}, u32[]{:S(2)}) collective-permute-start(f32[2,128]{1,0:T(2,128)S(1)} %get-tuple-element.33.step), channel_id=1, source_target_pairs={{1,2},{2,1},{3,4},{4,3},{5,6},{6,5},{7,8},{8,7},{9,10},{10,9},{11,... | collective-permute-start | bytes 3080 | tf_op jit(solution)/shard_map/ppermute | solution.py:306
